TPU v7x, 32 devices: a whole 2x2x4 slice. The times are simulated.
32 devices in a mesh: dp: 16 (over z, x, core), blk: 2 (over y).
Axes of the slice: x: 2, y: 2, z: 4, core: 2. Of those that a mesh axis runs over, the one named last changes fastest.
Arguments:
- patches: bfloat16 [16, 1024, 768], P('dp', 'blk'), may hold values from -6 to 6
- segments: int32 [16, 1024], P('dp'), may hold values from 0 to 34, as said below
- entry_gain: float32 [768], replicated, may hold values from 0.1 to 1.9
- entry_shift: float32 [768], replicated, may hold values from -3 to 3
- joint_weight: bfloat16 [768, 2304], replicated, may hold values from -0.21875 to 0.21875
- joint_bias: float32 [1536], replicated, may hold values from -3 to 3
- output_weight: bfloat16 [768, 768], replicated, may hold values from -0.625 to 0.625
- output_bias: float32 [768], replicated, may hold values from -3 to 3
- middle_gain: float32 [768], replicated, may hold values from 0.1 to 1.9
- middle_shift: float32 [768], replicated, may hold values from -3 to 3
- expand_weight: bfloat16 [768, 3072], replicated, may hold values from -0.21875 to 0.21875
- expand_bias: float32 [3072], replicated, may hold values from -3 to 3
- reduce_weight: bfloat16 [3072, 768], replicated, may hold values from -0.15625 to 0.15625
- reduce_bias: float32 [768], replicated, may hold values from -3 to 3
- cotangent: bfloat16 [16, 1024, 768], P('dp', 'blk'), may hold values from -6 to 6
Outputs:
- outputs: bfloat16 [16, 1024, 768], P('dp', 'blk')
- input_gradient: bfloat16 [16, 1024, 768], P('dp', 'blk')
- entry_gain_gradient: float32 [768], P('dp')
- entry_shift_gradient: float32 [768], P('dp')
- joint_weight_gradient: float32 [768, 2304], P('dp')
- joint_bias_gradient: float32 [1536], P('dp')
- output_weight_gradient: float32 [768, 768], P('dp')
- output_bias_gradient: float32 [768], P('dp')
- middle_gain_gradient: float32 [768], P('dp')
- middle_shift_gradient: float32 [768], P('dp')
- expand_weight_gradient: float32 [768, 3072], P('dp')
- expand_bias_gradient: float32 [3072], P('dp')
- reduce_weight_gradient: float32 [3072, 768], P('dp')
- reduce_bias_gradient: float32 [768], P('dp')
Inputs may be any that keep to these rules, and one draw needn't show every extreme that they name: `segments`: images are numbered 1, 2, ... in order and lie contiguously from position 0, each of 30 to 98 positions; the padding, 0, fills the end of every row with 1 to 98 positions.
All inputs are finite; a program needn't handle non-finite values.
Results may differ from a plain program's by a relative error of at most 0.019.
Values may be sent and summed in bfloat16 or wider, within the bound.
A program may use at most 192 MiB of HBM per device.

v0:
```python
import functools
import jax
import jax.numpy as jnp
from jax import lax
from jax.experimental import pallas as pl
from jax.experimental.pallas import tpu as pltpu
from jax.sharding import PartitionSpec as P

MESH = pl.DeviceIdType.MESH
CHUNKS = 18
BF = jnp.bfloat16
F32 = jnp.float32


class Grid:
    def __init__(self, dp, blk, width):
        self.A = 4
        self.B = dp // 8
        self.Y = blk
        self.dp = dp
        self.R = width // dp
        self.ny = 2 if blk == 2 else 0
        self.nx = 4 - self.ny


def comm_scratch(g):
    A, B, Y, R, nx, ny = g.A, g.B, g.Y, g.R, g.nx, g.ny
    shapes = dict(
        r0=pltpu.VMEM((CHUNKS, 4, B, A, R, 128), BF),
        rx=pltpu.VMEM((CHUNKS, B - 1, nx, A, R, 128), BF),
        rz=pltpu.VMEM((CHUNKS, A - 1, nx, R, 128), BF),
        ryx=pltpu.VMEM((CHUNKS, Y, nx, R, 128), BF),
        s_core=pltpu.SemaphoreType.DMA((2, CHUNKS)),
        s_x=pltpu.SemaphoreType.DMA((2, CHUNKS, B - 1)),
        s_z=pltpu.SemaphoreType.DMA((2, CHUNKS, A - 1)),
        s_yx=pltpu.SemaphoreType.DMA((2, CHUNKS, Y - 1)),
    )
    if ny:
        shapes.update(
            ry=pltpu.VMEM((CHUNKS, B, A, R, 128), BF),
            rx2=pltpu.VMEM((CHUNKS, B - 1, A, R, 128), BF),
            rz2=pltpu.VMEM((CHUNKS, A - 1, R, 128), BF),
            rag=pltpu.VMEM((CHUNKS, 2, R, 128), BF),
            s_y=pltpu.SemaphoreType.DMA((2, CHUNKS)),
            s_x2=pltpu.SemaphoreType.DMA((2, CHUNKS, B - 1)),
            s_z2=pltpu.SemaphoreType.DMA((2, CHUNKS, A - 1)),
            s_ag=pltpu.SemaphoreType.DMA((2, CHUNKS)),
        )
    return shapes


class Comm:
    def __init__(self, g, G, slots, refs, emit):
        self.g, self.G, self.slots, self.emit = g, G, slots, emit
        self.__dict__.update(refs)
        dp = lax.axis_index("dp")
        self.y = lax.axis_index("blk")
        self.c = dp % 2
        self.b = (dp // 2) % g.B
        self.a = dp // (2 * g.B)

    def dev(self, a=None, b=None, c=None, y=None):
        a = self.a if a is None else a
        b = self.b if b is None else b
        c = self.c if c is None else c
        y = self.y if y is None else y
        return ((a * self.g.B + b) * 2 + c, y)

    def partners(self):
        g = self.g
        return (
            [self.dev(c=1 - self.c)]
            + [self.dev(b=(self.b + k) % g.B) for k in range(1, g.B)]
            + [self.dev(a=(self.a + k) % g.A) for k in range(1, g.A)]
            + [self.dev(y=(self.y + k) % g.Y) for k in range(1, g.Y)]
        )

    def barrier(self):
        sem = pltpu.get_barrier_semaphore()
        others = self.partners()
        for other in others:
            pl.semaphore_signal(sem, inc=1, device_id=other, device_id_type=MESH)
        pl.semaphore_wait(sem, len(others))

    def copy(self, src, dst, sems, index, device):
        return pltpu.make_async_remote_copy(
            src_ref=src,
            dst_ref=dst,
            send_sem=sems.at[(0,) + index],
            recv_sem=sems.at[(1,) + index],
            device_id=device,
            device_id_type=MESH,
        )

    def stage0(self, j):
        s = j % self.slots
        return [self.copy(self.G.at[s, 1 - self.c], self.r0.at[j], self.s_core, (j,), self.dev(c=1 - self.c))]

    def stage1(self, j):
        g, s = self.g, j % self.slots
        out = []
        for k in range(1, g.B):
            other = (self.b + k) % g.B
            out.append(
                self.copy(
                    self.G.at[s, self.c, pl.ds(0, g.nx), other],
                    self.rx.at[j, k - 1],
                    self.s_x,
                    (j, k - 1),
                    self.dev(b=other),
                )
            )
        if g.ny:
            out.append(
                self.copy(
                    self.G.at[s, self.c, g.nx + 1 - self.y], self.ry.at[j], self.s_y, (j,), self.dev(y=1 - self.y)
                )
            )
        return out

    def stage2(self, j):
        g, s = self.g, j % self.slots
        out = []
        for k in range(1, g.A):
            other = (self.a + k) % g.A
            out.append(
                self.copy(
                    self.G.at[s, self.c, pl.ds(0, g.nx), self.b, other],
                    self.rz.at[j, k - 1],
                    self.s_z,
                    (j, k - 1),
                    self.dev(a=other),
                )
            )
        if g.ny:
            for k in range(1, g.B):
                other = (self.b + k) % g.B
                out.append(
                    self.copy(
                        self.G.at[s, self.c, g.nx + self.y, other],
                        self.rx2.at[j, k - 1],
                        self.s_x2,
                        (j, k - 1),
                        self.dev(b=other),
                    )
                )
        return out

    def stage3(self, j):
        g, s = self.g, j % self.slots
        out = []
        for k in range(1, g.Y):
            other = (self.y + k) % g.Y
            out.append(
                self.copy(
                    self.ryx.at[j, self.y], self.ryx.at[j, self.y], self.s_yx, (j, k - 1), self.dev(y=other)
                )
            )
        if g.ny:
            for k in range(1, g.A):
                other = (self.a + k) % g.A
                out.append(
                    self.copy(
                        self.G.at[s, self.c, g.nx + self.y, self.b, other],
                        self.rz2.at[j, k - 1],
                        self.s_z2,
                        (j, k - 1),
                        self.dev(a=other),
                    )
                )
        return out

    def stage4(self, j):
        if not self.g.ny:
            return []
        return [self.copy(self.rag.at[j, self.y], self.rag.at[j, self.y], self.s_ag, (j,), self.dev(y=1 - self.y))]

    def after0(self, j):
        s = j % self.slots
        g = self.g

        def add(i, _):
            col, b = i // g.B, i % g.B
            mine = self.G.at[s, self.c, col, b]
            mine[...] = mine[...] + self.r0[j, col, b]
            return 0

        lax.fori_loop(0, 4 * g.B, add, 0)

    def sum_into(self, mine, parts):
        total = mine[...].astype(F32)
        for part in parts:
            total = total + part.astype(F32)
        mine[...] = total.astype(BF)

    def after1(self, j):
        g, s = self.g, j % self.slots
        for col in range(g.nx):
            self.sum_into(
                self.G.at[s, self.c, col, self.b], [self.rx[j, k, col] for k in range(g.B - 1)]
            )
        if g.ny:
            for b in range(g.B):
                self.sum_into(self.G.at[s, self.c, g.nx + self.y, b], [self.ry[j, b]])

    def after2(self, j):
        g, s = self.g, j % self.slots
        total = self.G[s, self.c, pl.ds(0, g.nx), self.b, self.a].astype(F32)
        for k in range(g.A - 1):
            total = total + self.rz[j, k].astype(F32)
        self.ryx[j, self.y] = total.astype(BF)
        if g.ny:
            self.sum_into(
                self.G.at[s, self.c, g.nx + self.y, self.b], [self.rx2[j, k] for k in range(g.B - 1)]
            )

    def after3(self, j):
        g, s = self.g, j % self.slots
        total = self.ryx[j, 0].astype(F32)
        for k in range(1, g.Y):
            total = total + self.ryx[j, k].astype(F32)
        for col in range(g.nx):
            self.emit(j, col, total[col])
        if g.ny:
            total = self.G[s, self.c, g.nx + self.y, self.b, self.a].astype(F32)
            for k in range(g.A - 1):
                total = total + self.rz2[j, k].astype(F32)
            self.rag[j, self.y] = total.astype(BF)

    def after4(self, j):
        for k in range(self.g.ny):
            self.emit(j, self.g.nx + k, self.rag[j, k].astype(F32))

    def start(self, stage, j):
        for copy in (self.stage0, self.stage1, self.stage2, self.stage3, self.stage4)[stage](j):
            copy.start()

    def finish(self, stage, j):
        for copy in (self.stage0, self.stage1, self.stage2, self.stage3, self.stage4)[stage](j):
            copy.wait()
        (self.after0, self.after1, self.after2, self.after3, self.after4)[stage](j)
        if stage < 4:
            self.start(stage + 1, j)

    def advance(self, t, first=0, last=CHUNKS):
        for stage in range(4, -1, -1):
            j = t - stage
            if isinstance(j, int):
                if first <= j < last:
                    self.finish(stage, j)
            else:

                @pl.when((j >= first) & (j < last))
                def _(stage=stage, j=j):
                    self.finish(stage, j)


def emit_to(g, j_ref, o_ref, e_ref, r_ref):
    R = g.R

    def emit(j, col, value):
        @pl.when(j < 6)
        def _():
            e_ref[:, pl.ds(pl.multiple_of(j * 512 + col * 128, 128), 128)] = value

        @pl.when((j >= 6) & (j < 12))
        def _():
            r_ref[pl.ds(col * R, R), pl.ds(pl.multiple_of((j - 6) * 128, 128), 128)] = value

        @pl.when(j >= 12)
        def _():
            at = pl.multiple_of((j - 12) * 128, 128)
            if col < 3:
                j_ref[:, pl.ds(pl.multiple_of(col * 768 + at, 128), 128)] = value
            else:
                o_ref[:, pl.ds(at, 128)] = value

    return emit


HEADS = 12
HD = 64
D = 768
FF = 3072
ROWS = 512
EDGE = 128
SPAN = 3 * EDGE
PAIRS = HEADS // 2
SLOTS = 8
TICK = 512
TICKS = FF // TICK


def nn(left, right):
    return jnp.dot(left, right, preferred_element_type=F32)


def nt(left, right):
    return lax.dot_general(left, right, (((1,), (1,)), ((), ())), preferred_element_type=F32)


def stats(values):
    average = jnp.mean(values, axis=-1, keepdims=True)
    centred = values - average
    spread = jnp.mean(centred * centred, axis=-1, keepdims=True)
    inverse = lax.rsqrt(spread + 1e-06)
    return centred * inverse, inverse


def normal_parts(hidden):
    half = hidden * (0.5**0.5)
    size = jnp.abs(half)
    ratio = 1.0 / (1.0 + 0.3275911 * size)
    bell = jnp.exp(-half * half)
    tail = ((((1.061405429 * ratio - 1.453152027) * ratio + 1.421413741) * ratio - 0.284496736) * ratio + 0.254829592) * ratio
    tail = 0.5 * tail * bell
    share = jnp.where(hidden >= 0, 1.0 - tail, tail)
    return share, hidden * bell * 0.3989422804014327


def column_sum(values):
    return jnp.sum(values, axis=0, keepdims=True)


def layer_kernel(g, names, *refs):
    r = dict(zip(names, refs))
    A, B, R, Y = g.A, g.B, g.R, g.Y
    (patches, cotangent, segments, w_joint, w_output, w_expand, w_reduce) = (
        r[n] for n in ("patches", "cotangent", "segments", "w_joint", "w_output", "w_expand", "w_reduce")
    )
    G, vec = r["G"], r["vec"]
    r["oe"], r["oo"] = r["vT"], r["n2"]
    out_rows, dx_rows = r["k"].at[pl.ds(0, ROWS)], r["ml"]
    x, xh, dy = r["x"], r["xh"], r["dy"]
    comm = Comm(g, G, SLOTS, r, emit_to(g, r["j_out"], r["o_out"], r["e_out"], r["r_out"]))
    y = comm.y
    has_left, has_right = y > 0, y < Y - 1

    def load(src, dst, k):
        return pltpu.make_async_copy(src, dst, r["load"].at[k])

    load_x = load(patches, x, 0)
    load_wj = load(w_joint, r["wj"], 1)
    load_wo = load(w_output, r["wo"], 2)
    load_dy = load(cotangent, dy, 3)

    def ffn_loads(i):
        s = i % 3
        at = pl.ds(pl.multiple_of(i * TICK, TICK), TICK)
        return (
            pltpu.make_async_copy(w_expand.at[:, at], r["we"].at[s], r["stream"].at[0, s]),
            pltpu.make_async_copy(w_reduce.at[at], r["wr"].at[s], r["stream"].at[1, s]),
        )

    load_x.start()
    load_wj.start()
    load_wo.start()
    load_dy.start()
    for i in range(3):
        for copy in ffn_loads(i):
            copy.start()
    comm.barrier()

    def edge(k, side, src, dst, sems):
        other = comm.dev(y=(y + Y - 1) % Y) if side == 0 else comm.dev(y=(y + 1) % Y)
        return pltpu.make_async_remote_copy(
            src_ref=src, dst_ref=dst, send_sem=sems.at[(0,) + k + (side,)], recv_sem=sems.at[(1,) + k + (1 - side,)],
            device_id=other, device_id_type=MESH,
        )

    def x_edges():
        return (
            edge((), 0, patches.at[pl.ds(0, EDGE)], xh.at[1], r["s_edge"]),
            edge((), 1, patches.at[pl.ds(ROWS - EDGE, EDGE)], xh.at[0], r["s_edge"]),
        )

    to_left, to_right = x_edges()

    @pl.when(has_left)
    def _():
        to_left.start()

    @pl.when(has_right)
    def _():
        to_right.start()

    @pl.when(jnp.logical_not(has_left))
    def _():
        xh[0] = jnp.zeros((EDGE, D), BF)

    @pl.when(jnp.logical_not(has_right))
    def _():
        xh[1] = jnp.zeros((EDGE, D), BF)

    first_block = y * (ROWS // EDGE)
    count = segments.shape[0]
    columns = []
    for k in range(6):
        index = first_block + k - 1
        inside = (index >= 0) & (index < count)
        row = segments[pl.ds(jnp.clip(index, 0, count - 1), 1), :]
        row = jnp.where(inside, row, -1)
        columns.append(row)
    for b in range(4):
        for k in range(3):
            keys = jnp.broadcast_to(columns[b + k].astype(F32), (EDGE, EDGE)).T
            own = columns[b + 1].astype(F32)
            r["bias"][b, k * EDGE : (k + 1) * EDGE, :] = jnp.where(keys == own, 0.0, -1e30)

    vec[...] = jnp.zeros_like(vec)
    entry_gain, entry_shift = r["entry_gain"][...], r["entry_shift"][...]
    lanes = lax.broadcasted_iota(jnp.int32, (1, D), 1) % 128
    even = lanes < HD

    def project(rows, at, own, row_at):
        count = rows.shape[0]
        normal, _ = stats(rows.astype(F32))
        low = (normal * entry_gain + entry_shift).astype(BF)
        wj = r["wj"]
        key_rows = nn(low, wj[:, D : 2 * D]).astype(BF)
        r["k"][pl.ds(at, count), :] = key_rows
        r["kT"][:, pl.ds(at, count)] = key_rows.T
        value_rows = (nn(low, wj[:, 2 * D :]) + r["joint_bias"][:, D:]).astype(BF)
        r["v"][pl.ds(at, count), :] = value_rows
        r["vT"][:, pl.ds(at, count)] = value_rows.T
        if own:
            r["n1T"][:, pl.ds(row_at, count)] = low.T
            queries = (nn(low, wj[:, :D]) + r["joint_bias"][:, :D]).astype(BF) * BF(HD**-0.5)
            r["qe"][pl.ds(row_at, count), :] = jnp.where(even, queries, BF(0))
            r["qo"][pl.ds(row_at, count), :] = jnp.where(even, BF(0), queries)

    load_x.wait()
    load_wj.wait()

    def own_rows(i, _):
        at = pl.multiple_of(i * 256, 256)
        project(x[pl.ds(at, 256), :], pl.multiple_of(at + EDGE, EDGE), True, at)
        return 0

    lax.fori_loop(0, 2, own_rows, 0)

    @pl.when(has_left)
    def _():
        to_left.wait_send()
        to_right.wait_recv() if Y == 1 else edge((), 1, patches.at[pl.ds(0, EDGE)], xh.at[0], r["s_edge"]).wait_recv()

    @pl.when(has_right)
    def _():
        to_right.wait_send()
        edge((), 0, patches.at[pl.ds(0, EDGE)], xh.at[1], r["s_edge"]).wait_recv()

    def edge_rows(i, _):
        project(xh[i], pl.multiple_of(i * (ROWS + EDGE), EDGE), False, 0)
        return 0

    lax.fori_loop(0, 2, edge_rows, 0)

    top = lax.broadcasted_iota(jnp.int32, (EDGE, 1), 0) < HD

    def attend(p, _):
        at = pl.ds(pl.multiple_of(p * 128, 128), 128)
        for b in range(4):
            keys, own = pl.ds(b * EDGE, SPAN), pl.ds(b * EDGE, EDGE)
            both = jnp.concatenate([r["qe"][own, at], r["qo"][own, at]], axis=0)
            scores = nt(r["k"][keys, at], both)
            bias = r["bias"][b]
            scores = scores + jnp.concatenate([bias, bias], axis=1)
            powers = jnp.exp(scores - jnp.max(scores, axis=0, keepdims=True))
            probs = (powers * (1.0 / column_sum(powers))).astype(BF)
            r["probs"][p, b] = probs
            mixed = nn(r["vT"][at, keys], probs)
            r["attT"][at, own] = jnp.where(top, mixed[:, :128], mixed[:, 128:]).astype(BF)
        return 0

    lax.fori_loop(0, PAIRS, attend, 0)

    load_wo.wait()
    mid, total, n2, n2T = r["mid"], r["total"], r["n2"], r["n2T"]
    middle_gain, middle_shift = r["middle_gain"][...], r["middle_shift"][...]

    def finish_attention(i, _):
        at = pl.ds(pl.multiple_of(i * 256, 256), 256)
        mixed = r["attT"][:, at].T
        middle = x[at, :].astype(F32) + nn(mixed, r["wo"][...]) + r["output_bias"][...]
        mid[at, :] = middle
        total[at, :] = middle + r["reduce_bias"][...]
        normal, _ = stats(middle)
        low = (normal * middle_gain + middle_shift).astype(BF)
        n2[at, :] = low
        n2T[:, at] = low.T
        r["dn"][at, :] = jnp.zeros((256, D), F32)
        return 0

    lax.fori_loop(0, 2, finish_attention, 0)
    load_dy.wait()

    def feed_forward(i, _):
        s = i % 3
        for copy in ffn_loads(i):
            copy.wait()
        we, wr = r["we"].at[s], r["wr"].at[s]
        at = pl.ds(pl.multiple_of(i * TICK, TICK), TICK)
        bias = r["expand_bias"][:, at]
        bias_sum = jnp.zeros((1, TICK), F32)
        for half in range(2):
            rows = pl.ds(half * 256, 256)
            hidden = nn(n2[rows, :], we[...]) + bias
            back = nt(dy[rows, :], wr[...])
            share, slope = normal_parts(hidden)
            active = (hidden * share).astype(BF)
            hidden_gradient = back * (share + slope)
            bias_sum = bias_sum + column_sum(hidden_gradient)
            low = hidden_gradient.astype(BF)
            r["hl"][rows, :] = low
            r["actT"][at, rows] = active.T
            total[rows, :] += nn(active, wr[...])
            r["dn"][rows, :] += nt(low, we[...])
        r["eb"][:, at] = bias_sum
        for part in range(2):
            block = nn(n2T[part * 384 : (part + 1) * 384, :], r["hl"][...]).astype(BF)
            store_rows(block, i, part * 2, 2)
        comm.start(0, i)

        @pl.when(i + 3 < TICKS)
        def _():
            for copy in ffn_loads(i + 3):
                copy.start()

        comm.advance(i - 1)
        return 0

    def store_rows(block, chunk, a0, na):
        slot = chunk % SLOTS
        for a in range(na):
            for b in range(B):
                for c in range(2):
                    row = ((a * B + b) * 2 + c) * R
                    for col in range(block.shape[1] // 128):
                        G[slot, c, col, b, a0 + a] = block[row : row + R, col * 128 : (col + 1) * 128]

    lax.fori_loop(0, TICKS, feed_forward, 0)

    def reduce_gradient(p, _):
        at = pl.ds(pl.multiple_of(p * 256, 256), 256)
        chunk = 6 + 2 * p

        def part(a, _):
            block = nn(r["actT"][pl.ds(pl.multiple_of(a * D, D), D), :], dy[:, at]).astype(BF)
            for h in range(2):
                slot = (chunk + h) % SLOTS
                for b in range(B):
                    for c in range(2):
                        for k in range(4):
                            row = ((b * 2 + c) * 4 + k) * R
                            G[slot, c, k, b, a] = block[row : row + R, h * 128 : (h + 1) * 128]
            return 0

        lax.fori_loop(0, A, part, 0)
        comm.start(0, chunk)
        comm.start(0, chunk + 1)
        comm.advance(5 + p)
        return 0

    lax.fori_loop(0, 3, reduce_gradient, 0)

    def middle_back(i, _):
        at = pl.ds(pl.multiple_of(i * 256, 256), 256)
        out_rows[at, :] = total[at, :].astype(BF)
        error = r["dn"][at, :]
        normal, inverse = stats(mid[at, :])
        scaled = error * middle_gain
        part = inverse * (
            scaled
            - jnp.mean(scaled, axis=-1, keepdims=True)
            - normal * jnp.mean(scaled * normal, axis=-1, keepdims=True)
        )
        incoming = dy[at, :].astype(F32)
        gradient = incoming + part
        vec[5:6, :] += column_sum(error * normal)
        vec[6:7, :] += column_sum(error)
        vec[4:5, :] += column_sum(gradient)
        vec[11:12, :] += column_sum(incoming)
        mid[at, :] = gradient
        low = gradient.astype(BF)
        r["ml"][at, :] = low
        back = nt(low, r["wo"][...]).astype(BF)
        r["oe"][at, :] = jnp.where(even, back, BF(0))
        r["oo"][at, :] = jnp.where(even, BF(0), back)
        total[at, :] = jnp.zeros((256, D), F32)
        return 0

    lax.fori_loop(0, 2, middle_back, 0)
    save_out = pltpu.make_async_copy(out_rows, r["out"], r["save"].at[0])
    save_out.start()
    for k in range(4):
        vec[7 + k : 8 + k, :] = r["eb"][:, k * D : (k + 1) * D]
    comm.advance(8)

    parts, jq, sent, got, s_part = r["parts"], r["jq"], r["sent"], r["got"], r["s_part"]

    def part_copies(p):
        return (
            edge((p,), 0, sent.at[p % 2, 0], got.at[p, 1], s_part),
            edge((p,), 1, sent.at[p % 2, 1], got.at[p, 0], s_part),
        )

    def attend_back(p):
        at = pl.ds(pl.multiple_of(p * 128, 128), 128)
        slot = p % 2
        own_sum = jnp.zeros((1, 128), F32)
        parts[slot] = jnp.zeros((ROWS + 2 * EDGE, 256), F32)
        for b in range(4):
            keys, own = pl.ds(b * EDGE, SPAN), pl.ds(b * EDGE, EDGE)
            queries = jnp.concatenate([r["qe"][own, at], r["qo"][own, at]], axis=0)
            errors = jnp.concatenate([r["oe"][own, at], r["oo"][own, at]], axis=0)
            shares = nt(r["v"][keys, at], errors)
            probs = r["probs"][p, b]
            wide = probs.astype(F32)
            product = wide * shares
            delta = column_sum(product)
            low = (product - wide * delta).astype(BF)
            parts[slot, keys, 0:128] += nn(low, queries)
            parts[slot, keys, 128:256] += nn(probs, errors)
            turned = nn(r["kT"][at, keys], low)
            mine = (jnp.where(top, turned[:, :128], turned[:, 128:]) * HD**-0.5).T
            own_sum = own_sum + column_sum(mine)
            jq[slot, own, :] = mine.astype(BF)
        vec[2:3, at] = own_sum
        to_left, to_right = part_copies(p)

        @pl.when(has_left)
        def _():
            sent[slot, 0] = parts[slot, 0:EDGE, :].astype(BF)
            to_left.start()

        @pl.when(has_right)
        def _():
            sent[slot, 1] = parts[slot, ROWS + EDGE :, :].astype(BF)
            to_right.start()

    def joint_gradient(p):
        at = pl.ds(pl.multiple_of(p * 128, 128), 128)
        slot = p % 2
        to_left, to_right = part_copies(p)

        @pl.when(has_left)
        def _():
            to_left.wait_send()
            to_right.wait_recv()
            parts[slot, EDGE : 2 * EDGE, :] += got[p, 0].astype(F32)

        @pl.when(has_right)
        def _():
            to_right.wait_send()
            to_left.wait_recv()
            parts[slot, ROWS : ROWS + EDGE, :] += got[p, 1].astype(F32)

        sums = parts[slot, EDGE : ROWS + EDGE, :]
        vec[3:4, at] = column_sum(sums[:, 128:])
        low = jnp.concatenate([jq[slot], sums.astype(BF)], axis=1)
        wj = r["wj"]
        weights = jnp.concatenate([wj[:, pl.ds(pl.multiple_of(k * D + p * 128, 128), 128)] for k in range(3)], axis=1)
        total[...] += nt(low, weights)
        low_out = r["ml"][:, at]
        for part in range(2):
            rows = pl.ds(part * 384, 384)
            block = nn(r["n1T"][rows, :], low).astype(BF)
            block_out = nn(r["attT"][rows, :], low_out).astype(BF)
            store_rows(jnp.concatenate([block, block_out], axis=1), 12 + p, part * 2, 2)
        comm.start(0, 12 + p)

    def pair_step(i, _):
        @pl.when(i < PAIRS)
        def _():
            attend_back(i)

        @pl.when(i > 0)
        def _():
            joint_gradient(i - 1)

        comm.advance(9 + i)
        return 0

    lax.fori_loop(0, PAIRS + 1, pair_step, 0)

    def entry_back(i, _):
        at = pl.ds(pl.multiple_of(i * 256, 256), 256)
        error = total[at, :]
        normal, inverse = stats(x[at, :].astype(F32))
        scaled = error * entry_gain
        part = inverse * (
            scaled
            - jnp.mean(scaled, axis=-1, keepdims=True)
            - normal * jnp.mean(scaled * normal, axis=-1, keepdims=True)
        )
        vec[0:1, :] += column_sum(error * normal)
        vec[1:2, :] += column_sum(error)
        dx_rows[at, :] = (mid[at, :] + part).astype(BF)
        return 0

    lax.fori_loop(0, 2, entry_back, 0)
    save_dx = pltpu.make_async_copy(dx_rows, r["dx"], r["save"].at[1])
    save_dx.start()

    rv, s_vec = r["rv"], r["s_vec"]

    def vector_copies(step):
        groups = (
            [comm.dev(c=1 - comm.c)],
            [comm.dev(b=(comm.b + k) % B) for k in range(1, B)],
            [comm.dev(a=(comm.a + k) % A) for k in range(1, A)],
            [comm.dev(y=(comm.y + k) % Y) for k in range(1, Y)],
        )
        ids = (comm.c, comm.b, comm.a, comm.y)
        base = (0, 2, 2 + B, 2 + B + A)[step]
        here = rv.at[base + ids[step]]
        return here, [
            comm.copy(here, here, s_vec, (base + k,), other) for k, other in enumerate(groups[step])
        ]

    def vector_sum(step):
        base, size = ((0, 2), (2, B), (2 + B, A), (2 + B + A, Y))[step]
        value = rv[base]
        for k in range(1, size):
            value = value + rv[base + k]
        return value

    def vector_start(step, value):
        here, copies = vector_copies(step)
        here[...] = value
        for copy in copies:
            copy.start()

    def vector_wait(step):
        for copy in vector_copies(step)[1]:
            copy.wait()

    vector_start(0, vec[...])
    for step in range(4):
        comm.advance(16 + step)
        vector_wait(step)
        if step < 3:
            vector_start(step + 1, vector_sum(step))
    summed = vector_sum(3)
    place = lax.axis_index("dp")
    spot = lax.broadcasted_iota(jnp.int32, (D, 512), 0)
    lane = lax.broadcasted_iota(jnp.int32, (D, 512), 1)
    n2v, n4v = g.dp // 2, g.dp // 4
    want = jnp.where(
        lane < 128,
        lane + place * R,
        jnp.where(lane < 256, lane - 128 + (place % n2v) * (2 * R), lane - 256 + (place % n4v) * (4 * R)),
    )
    pick = jnp.where(spot == want, 1.0, 0.0).astype(F32)
    picked = jnp.dot(summed, pick, precision=lax.Precision.HIGHEST, preferred_element_type=F32)
    kind = lax.broadcasted_iota(jnp.int32, (16, 1), 0)
    r["v_out"][...] = picked[:, 0:128]
    r["jb_out"][...] = column_sum(jnp.where(kind == 2 + place // n2v, picked[:, 128:256], 0.0))
    r["eb_out"][...] = column_sum(jnp.where(kind == 7 + place // n4v, picked[:, 256:512], 0.0))
    for t in range(20, CHUNKS + 4):
        comm.advance(t)
    save_out.wait()
    save_dx.wait()


def layer(g, patches, segments, vectors, weights, cotangent):
    A, B, R, Y = g.A, g.B, g.R, g.Y
    comm_shapes = comm_scratch(g)
    V = pl.BlockSpec(memory_space=pltpu.VMEM)
    H = pl.BlockSpec(memory_space=pl.ANY)
    inputs = dict(
        patches=(patches, H),
        cotangent=(cotangent, H),
        segments=(segments, V),
        w_joint=(weights[0], H),
        w_output=(weights[1], H),
        w_expand=(weights[2], H),
        w_reduce=(weights[3], H),
        **{name: (value, V) for name, value in vectors.items()},
    )
    outputs = dict(
        out=((ROWS, D), BF),
        dx=((ROWS, D), BF),
        j_out=((R, 3 * D), F32),
        o_out=((R, D), F32),
        e_out=((R, FF), F32),
        r_out=((4 * R, D), F32),
        v_out=((16, 128), F32),
        jb_out=((1, 128), F32),
        eb_out=((1, 256), F32),
    )
    ext = ROWS + 2 * EDGE
    scratch = dict(
        x=pltpu.VMEM((ROWS, D), BF),
        xh=pltpu.VMEM((2, EDGE, D), BF),
        dy=pltpu.VMEM((ROWS, D), BF),
        wj=pltpu.VMEM((D, 3 * D), BF),
        wo=pltpu.VMEM((D, D), BF),
        we=pltpu.VMEM((3, D, TICK), BF),
        wr=pltpu.VMEM((3, TICK, D), BF),
        n1T=pltpu.VMEM((D, ROWS), BF),
        qe=pltpu.VMEM((ROWS, D), BF),
        qo=pltpu.VMEM((ROWS, D), BF),
        k=pltpu.VMEM((ext, D), BF),
        v=pltpu.VMEM((ext, D), BF),
        kT=pltpu.VMEM((D, ext), BF),
        vT=pltpu.VMEM((D, ext), BF),
        bias=pltpu.VMEM((4, SPAN, EDGE), F32),
        probs=pltpu.VMEM((PAIRS, 4, SPAN, 2 * EDGE), BF),
        attT=pltpu.VMEM((D, ROWS), BF),
        mid=pltpu.VMEM((ROWS, D), F32),
        total=pltpu.VMEM((ROWS, D), F32),
        dn=pltpu.VMEM((ROWS, D), F32),
        n2=pltpu.VMEM((ROWS, D), BF),
        n2T=pltpu.VMEM((D, ROWS), BF),
        hl=pltpu.VMEM((ROWS, TICK), BF),
        actT=pltpu.VMEM((FF, ROWS), BF),
        eb=pltpu.VMEM((1, FF), F32),
        ml=pltpu.VMEM((ROWS, D), BF),
        parts=pltpu.VMEM((2, ext, 256), F32),
        jq=pltpu.VMEM((2, ROWS, 128), BF),
        sent=pltpu.VMEM((2, 2, EDGE, 256), BF),
        got=pltpu.VMEM((PAIRS, 2, EDGE, 256), BF),
        vec=pltpu.VMEM((16, D), F32),
        rv=pltpu.VMEM((2 + B + A + Y, 16, D), F32),
        G=pltpu.VMEM((SLOTS, 2, 4, B, A, R, 128), BF),
        load=pltpu.SemaphoreType.DMA((4,)),
        save=pltpu.SemaphoreType.DMA((2,)),
        stream=pltpu.SemaphoreType.DMA((2, 3)),
        s_edge=pltpu.SemaphoreType.DMA((2, 2)),
        s_part=pltpu.SemaphoreType.DMA((2, PAIRS, 2)),
        s_vec=pltpu.SemaphoreType.DMA((2, 2 + B + A + Y)),
        **comm_shapes,
    )
    names = (*inputs, *outputs, *scratch)
    results = pl.pallas_call(
        functools.partial(layer_kernel, g, names),
        out_shape=tuple(jax.ShapeDtypeStruct(*shape) for shape in outputs.values()),
        in_specs=[spec for _, spec in inputs.values()],
        out_specs=[H, H] + [V] * (len(outputs) - 2),
        scratch_shapes=list(scratch.values()),
        compiler_params=pltpu.CompilerParams(
            collective_id=0, has_side_effects=True, vmem_limit_bytes=64 << 20
        ),
    )(*(value for value, _ in inputs.values()))
    return dict(zip(outputs, results))


def local(
    patches,
    segments,
    entry_gain,
    entry_shift,
    joint_weight,
    joint_bias,
    output_weight,
    output_bias,
    middle_gain,
    middle_shift,
    expand_weight,
    expand_bias,
    reduce_weight,
    reduce_bias,
    cotangent,
):
    g = Grid(lax.axis_size("dp"), lax.axis_size("blk"), D)
    R = g.R
    vectors = dict(
        entry_gain=entry_gain,
        entry_shift=entry_shift,
        joint_bias=joint_bias,
        output_bias=output_bias,
        middle_gain=middle_gain,
        middle_shift=middle_shift,
        expand_bias=expand_bias,
        reduce_bias=reduce_bias,
    )
    o = layer(
        g,
        patches[0],
        segments.reshape(-1, EDGE),
        {name: value.reshape(1, -1) for name, value in vectors.items()},
        (joint_weight, output_weight, expand_weight, reduce_weight),
        cotangent[0],
    )
    v = o["v_out"]
    return (
        o["out"][None],
        o["dx"][None],
        v[0, :R],
        v[1, :R],
        o["j_out"],
        o["jb_out"][0, : 2 * R],
        o["o_out"],
        v[4, :R],
        v[5, :R],
        v[6, :R],
        o["e_out"],
        o["eb_out"][0, : 4 * R],
        o["r_out"],
        v[11, :R],
    )


def solution(mesh):
    return jax.shard_map(
        local,
        mesh=mesh,
        in_specs=(
            P("dp", "blk", None),
            P("dp", None),
            P(),
            P(),
            P(),
            P(),
            P(),
            P(),
            P(),
            P(),
            P(),
            P(),
            P(),
            P(),
            P("dp", "blk", None),
        ),
        out_specs=(
            P("dp", "blk", None),
            P("dp", "blk", None),
            P("dp"),
            P("dp"),
            P("dp", None),
            P("dp"),
            P("dp", None),
            P("dp"),
            P("dp"),
            P("dp"),
            P("dp", None),
            P("dp"),
            P("dp", None),
            P("dp"),
        ),
        check_vma=False,
    )
```

profile of v0, /device:TPU:0, one launch (start us, length us, event | category | flops | bytes accessed | tf_op | source)
XLA Modules:
  0.0 158.6 jit_solution(13762662518095563166)
XLA Ops:
  0.6 1.3 reshape.58.refs_9_
  1.9 1.3 reshape.56.refs_7_
  3.2 1.3 reshape.57.refs_8_
  4.5 1.3 reshape.59.refs_10_
  5.7 1.3 reshape.60.refs_11_
  7.0 1.3 reshape.61.refs_12_
  8.3 1.3 reshape.63.refs_14_
  9.6 136.8 %shard_map.254 = (bf16[512,768]{1,0:T(8,128)(2,1)}, bf16[512,768]{1,0:T(8,128)(2,1)}, f32[48,2304]{1,0:T(8,128)}, f32[48,768]{1,0:T(8,128)}, f32[48,3072]{1,0:T(...) custom-call(bf16[512,768]{1,0:T(8,128)(2,1)} %bitcast.22, ...), custom_call_target="tpu_custom_call" | custom-call | tf_op jit(solution)/shard_map/pallas_call | solution.py:836
  146.4 0.0 copy-start.1
  146.4 0.0 copy-start.2
  146.4 0.0 copy-start
  146.4 1.4 slice_bitcast_fusion
  147.8 1.1 slice_bitcast_fusion.4
  148.9 2.1 %copy.36 = bf16[1,512,768]{2,1,0:T(8,128)(2,1)} copy(bf16[1,512,768]{2,1,0:T(8,128)(2,1)} %bitcast.25) | data formatting | bytes 1572864
  151.0 2.1 %copy.37 = bf16[1,512,768]{2,1,0:T(8,128)(2,1)} copy(bf16[1,512,768]{2,1,0:T(8,128)(2,1)} %bitcast.24) | data formatting | bytes 1572864
  153.0 1.8 %copy.38 = f32[48,2304]{1,0:T(8,128)} copy(f32[48,2304]{1,0:T(8,128)} %get-tuple-element.56) | data formatting | bytes 884736
  154.8 1.6 copy.39
  156.4 0.0 copy-done.1
  156.4 0.8 copy.40
  157.2 0.0 copy-done.2
  157.2 0.6 copy.41
  157.8 0.0 copy-done
  157.8 0.8 copy.42
Async XLA Ops:
  146.4 10.0 %copy-start.1 = (f32[48,3072]{1,0:T(8,128)S(1)}, f32[48,3072]{1,0:T(8,128)}, u32[]{:S(2)}) copy-start(f32[48,3072]{1,0:T(8,128)} %get-tuple-element.62) | copy-start | bytes 1769476
  146.4 10.8 %copy-start.2 = (f32[1,256]{1,0:T(1,128)S(1)}, f32[1,256]{1,0:T(1,128)}, u32[]{:S(2)}) copy-start(f32[1,256]{1,0:T(1,128)} %get-tuple-element.30) | copy-start | bytes 3076
  146.4 11.4 %copy-start = (f32[192,768]{1,0:T(8,128)S(1)}, f32[192,768]{1,0:T(8,128)}, u32[]{:S(2)}) copy-start(f32[192,768]{1,0:T(8,128)} %get-tuple-element.64) | copy-start | bytes 1769476
where the time goes:
time: 159 us
  Pallas kernels  137 us (86%)
  local copies, waits for them, and re-layouts  21.1 us (13%)
    pallas_call x1, Pallas kernels, layer(): pl.pallas_call(functools.partial(layer_kernel, g, names), out_shape=tuple...  137 us
    unnamed x13, local copies, waits for them, and re-layouts  9.71 us
    reshape x7, local copies, waits for them, and re-layouts, local(): value.reshape(1, -1)  8.91 us

commit v1 on v0

--- a/solution.py
+++ b/solution.py
@@ -8,6 +8,8 @@
 
 MESH = pl.DeviceIdType.MESH
 CHUNKS = 18
+LAG = 2
+RING = 9
 BF = jnp.bfloat16
 F32 = jnp.float32
 
@@ -26,7 +28,7 @@
 def comm_scratch(g):
     A, B, Y, R, nx, ny = g.A, g.B, g.Y, g.R, g.nx, g.ny
     shapes = dict(
-        r0=pltpu.VMEM((CHUNKS, 4, B, A, R, 128), BF),
+        r0=pltpu.VMEM((RING, 4, B, A, R, 128), BF),
         rx=pltpu.VMEM((CHUNKS, B - 1, nx, A, R, 128), BF),
         rz=pltpu.VMEM((CHUNKS, A - 1, nx, R, 128), BF),
         ryx=pltpu.VMEM((CHUNKS, Y, nx, R, 128), BF),
@@ -94,7 +96,7 @@
 
     def stage0(self, j):
         s = j % self.slots
-        return [self.copy(self.G.at[s, 1 - self.c], self.r0.at[j], self.s_core, (j,), self.dev(c=1 - self.c))]
+        return [self.copy(self.G.at[s, 1 - self.c], self.r0.at[j % RING], self.s_core, (j,), self.dev(c=1 - self.c))]
 
     def stage1(self, j):
         g, s = self.g, j % self.slots
@@ -182,7 +184,7 @@
         def add(i, _):
             col, b = i // g.B, i % g.B
             mine = self.G.at[s, self.c, col, b]
-            mine[...] = mine[...] + self.r0[j, col, b]
+            mine[...] = mine[...] + self.r0[j % RING, col, b]
             return 0
 
         lax.fori_loop(0, 4 * g.B, add, 0)
@@ -244,7 +246,7 @@
 
     def advance(self, t, first=0, last=CHUNKS):
         for stage in range(4, -1, -1):
-            j = t - stage
+            j = t - LAG * stage
             if isinstance(j, int):
                 if first <= j < last:
                     self.finish(stage, j)
@@ -279,6 +281,10 @@
 
 
 HEADS = 12
+VECTORS = (
+    "entry_gain", "entry_shift", "joint_bias", "output_bias",
+    "middle_gain", "middle_shift", "expand_bias", "reduce_bias",
+)
 HD = 64
 D = 768
 FF = 3072
@@ -286,7 +292,8 @@
 EDGE = 128
 SPAN = 3 * EDGE
 PAIRS = HEADS // 2
-SLOTS = 8
+SLOTS = 12
+STREAM = 2
 TICK = 512
 TICKS = FF // TICK
 
@@ -329,6 +336,9 @@
         r[n] for n in ("patches", "cotangent", "segments", "w_joint", "w_output", "w_expand", "w_reduce")
     )
     G, vec = r["G"], r["vec"]
+    for name in VECTORS:
+        r[name + "_row"][...] = r[name][...].reshape(1, -1)
+        r[name] = r[name + "_row"]
     r["oe"], r["oo"] = r["vT"], r["n2"]
     out_rows, dx_rows = r["k"].at[pl.ds(0, ROWS)], r["ml"]
     x, xh, dy = r["x"], r["xh"], r["dy"]
@@ -345,7 +355,7 @@
     load_dy = load(cotangent, dy, 3)
 
     def ffn_loads(i):
-        s = i % 3
+        s = i % STREAM
         at = pl.ds(pl.multiple_of(i * TICK, TICK), TICK)
         return (
             pltpu.make_async_copy(w_expand.at[:, at], r["we"].at[s], r["stream"].at[0, s]),
@@ -354,11 +364,6 @@
 
     load_x.start()
     load_wj.start()
-    load_wo.start()
-    load_dy.start()
-    for i in range(3):
-        for copy in ffn_loads(i):
-            copy.start()
     comm.barrier()
 
     def edge(k, side, src, dst, sems):
@@ -431,6 +436,11 @@
 
     load_x.wait()
     load_wj.wait()
+    load_wo.start()
+    load_dy.start()
+    for i in range(STREAM):
+        for copy in ffn_loads(i):
+            copy.start()
 
     def own_rows(i, _):
         at = pl.multiple_of(i * 256, 256)
@@ -495,7 +505,7 @@
     load_dy.wait()
 
     def feed_forward(i, _):
-        s = i % 3
+        s = i % STREAM
         for copy in ffn_loads(i):
             copy.wait()
         we, wr = r["we"].at[s], r["wr"].at[s]
@@ -521,9 +531,9 @@
             store_rows(block, i, part * 2, 2)
         comm.start(0, i)
 
-        @pl.when(i + 3 < TICKS)
+        @pl.when(i + STREAM < TICKS)
         def _():
-            for copy in ffn_loads(i + 3):
+            for copy in ffn_loads(i + STREAM):
                 copy.start()
 
         comm.advance(i - 1)
@@ -712,22 +722,24 @@
             [comm.dev(y=(comm.y + k) % Y) for k in range(1, Y)],
         )
         ids = (comm.c, comm.b, comm.a, comm.y)
-        base = (0, 2, 2 + B, 2 + B + A)[step]
-        here = rv.at[base + ids[step]]
+        base = (0, 2, 0, A)[step]
+        held = rv if step < 2 else r["rvl"]
+        here = held.at[base + ids[step]]
         return here, [
-            comm.copy(here, here, s_vec, (base + k,), other) for k, other in enumerate(groups[step])
+            comm.copy(here, here, s_vec, ((0, 2, 2 + B, 2 + B + A)[step] + k,), other) for k, other in enumerate(groups[step])
         ]
 
     def vector_sum(step):
-        base, size = ((0, 2), (2, B), (2 + B, A), (2 + B + A, Y))[step]
-        value = rv[base]
+        base, size = ((0, 2), (2, B), (0, A), (A, Y))[step]
+        held = rv if step < 2 else r["rvl"]
+        value = held[base].astype(F32)
         for k in range(1, size):
-            value = value + rv[base + k]
+            value = value + held[base + k].astype(F32)
         return value
 
     def vector_start(step, value):
         here, copies = vector_copies(step)
-        here[...] = value
+        here[...] = value.astype(here.dtype)
         for copy in copies:
             copy.start()
 
@@ -757,7 +769,7 @@
     r["v_out"][...] = picked[:, 0:128]
     r["jb_out"][...] = column_sum(jnp.where(kind == 2 + place // n2v, picked[:, 128:256], 0.0))
     r["eb_out"][...] = column_sum(jnp.where(kind == 7 + place // n4v, picked[:, 256:512], 0.0))
-    for t in range(20, CHUNKS + 4):
+    for t in range(20, CHUNKS + 4 * LAG):
         comm.advance(t)
     save_out.wait()
     save_dx.wait()
@@ -796,8 +808,8 @@
         dy=pltpu.VMEM((ROWS, D), BF),
         wj=pltpu.VMEM((D, 3 * D), BF),
         wo=pltpu.VMEM((D, D), BF),
-        we=pltpu.VMEM((3, D, TICK), BF),
-        wr=pltpu.VMEM((3, TICK, D), BF),
+        we=pltpu.VMEM((STREAM, D, TICK), BF),
+        wr=pltpu.VMEM((STREAM, TICK, D), BF),
         n1T=pltpu.VMEM((D, ROWS), BF),
         qe=pltpu.VMEM((ROWS, D), BF),
         qo=pltpu.VMEM((ROWS, D), BF),
@@ -822,14 +834,16 @@
         sent=pltpu.VMEM((2, 2, EDGE, 256), BF),
         got=pltpu.VMEM((PAIRS, 2, EDGE, 256), BF),
         vec=pltpu.VMEM((16, D), F32),
-        rv=pltpu.VMEM((2 + B + A + Y, 16, D), F32),
+        rv=pltpu.VMEM((2 + B, 16, D), F32),
+        rvl=pltpu.VMEM((A + Y, 16, D), BF),
         G=pltpu.VMEM((SLOTS, 2, 4, B, A, R, 128), BF),
         load=pltpu.SemaphoreType.DMA((4,)),
         save=pltpu.SemaphoreType.DMA((2,)),
-        stream=pltpu.SemaphoreType.DMA((2, 3)),
+        stream=pltpu.SemaphoreType.DMA((2, STREAM)),
         s_edge=pltpu.SemaphoreType.DMA((2, 2)),
         s_part=pltpu.SemaphoreType.DMA((2, PAIRS, 2)),
         s_vec=pltpu.SemaphoreType.DMA((2, 2 + B + A + Y)),
+        **{name + "_row": pltpu.VMEM((1, value.shape[0]), F32) for name, value in vectors.items()},
         **comm_shapes,
     )
     names = (*inputs, *outputs, *scratch)
@@ -843,7 +857,40 @@
             collective_id=0, has_side_effects=True, vmem_limit_bytes=64 << 20
         ),
     )(*(value for value, _ in inputs.values()))
-    return dict(zip(outputs, results))
+    return hand_over(g, dict(zip(outputs, results)))
+
+
+def hand_over_kernel(g, out, dx, j, o, e, w, v, jb, eb, *refs):
+    outs, sems = refs[:14], refs[14]
+    R = g.R
+    moves = [(out, 0), (dx, 1), (j, 4), (o, 6), (e, 10), (w, 12)]
+    copies = [pltpu.make_async_copy(src, outs[k], sems.at[i]) for i, (src, k) in enumerate(moves)]
+    for copy in copies:
+        copy.start()
+    for row, k in ((0, 2), (1, 3), (4, 7), (5, 8), (6, 9), (11, 13)):
+        outs[k][...] = v[row, :R]
+    outs[5][...] = jb[0, : 2 * R]
+    outs[11][...] = eb[0, : 4 * R]
+    for copy in copies:
+        copy.wait()
+
+
+def hand_over(g, o):
+    R = g.R
+    V = pl.BlockSpec(memory_space=pltpu.VMEM)
+    H = pl.BlockSpec(memory_space=pl.ANY)
+    shapes = [
+        ((ROWS, D), BF), ((ROWS, D), BF), ((R,), F32), ((R,), F32), ((R, 3 * D), F32), ((2 * R,), F32), ((R, D), F32),
+        ((R,), F32), ((R,), F32), ((R,), F32), ((R, FF), F32), ((4 * R,), F32), ((4 * R, D), F32), ((R,), F32),
+    ]
+    names = ("out", "dx", "j_out", "o_out", "e_out", "r_out", "v_out", "jb_out", "eb_out")
+    return pl.pallas_call(
+        functools.partial(hand_over_kernel, g),
+        out_shape=tuple(jax.ShapeDtypeStruct(*shape) for shape in shapes),
+        in_specs=[V] * 9,
+        out_specs=[V if len(shape) == 1 else H for shape, _ in shapes],
+        scratch_shapes=[pltpu.SemaphoreType.DMA((6,))],
+    )(*(o[name] for name in names))
 
 
 def local(
@@ -879,27 +926,11 @@
         g,
         patches[0],
         segments.reshape(-1, EDGE),
-        {name: value.reshape(1, -1) for name, value in vectors.items()},
+        vectors,
         (joint_weight, output_weight, expand_weight, reduce_weight),
         cotangent[0],
     )
-    v = o["v_out"]
-    return (
-        o["out"][None],
-        o["dx"][None],
-        v[0, :R],
-        v[1, :R],
-        o["j_out"],
-        o["jb_out"][0, : 2 * R],
-        o["o_out"],
-        v[4, :R],
-        v[5, :R],
-        v[6, :R],
-        o["e_out"],
-        o["eb_out"][0, : 4 * R],
-        o["r_out"],
-        v[11, :R],
-    )
+    return (o[0][None], o[1][None], *o[2:])
 
 
 def solution(mesh):

time: 159 us -> 123 us (0.77)
  local copies, waits for them, and re-layouts: 21.1 us -> 0 us
  Pallas kernels: 137 us -> 122 us
    pallas_call x1, Pallas kernels: 137 us -> 118 us  [layer(): pl.pallas_call(functools.partial(layer_kernel, g, names), out_shape=tuple...]
    unnamed x13 -> x0, local copies, waits for them, and re-layouts: 9.71 us -> none
    reshape x7 -> x0, local copies, waits for them, and re-layouts: 8.91 us -> none  [local(): value.reshape(1, -1)]
    pallas_call x0 -> x1, Pallas kernels: none -> 4.28 us  [hand_over(): pl.pallas_call(functools.partial(hand_over_kernel, g), out_shape=tuple((j...]
    squeeze x2 -> x0, local copies, waits for them, and re-layouts: 2.47 us -> none  [the longest x1 1.36 us: local(): v[11, :R]]
where the time goes in v1:
time: 123 us
  Pallas kernels  122 us (99%)
    pallas_call x1, Pallas kernels, layer(): pl.pallas_call(functools.partial(layer_kernel, g, names), out_shape=tuple...  118 us
    pallas_call x1, Pallas kernels, hand_over(): pl.pallas_call(functools.partial(hand_over_kernel, g), out_shape=tuple((j...  4.28 us

profile of v1, /device:TPU:0, one launch (start us, length us, event | category | flops | bytes accessed | tf_op | source)
XLA Modules:
  0.0 123.3 jit_solution(7073992108819493892)
XLA Ops:
  0.7 118.2 %shard_map.254 = (bf16[512,768]{1,0:T(8,128)(2,1)}, bf16[512,768]{1,0:T(8,128)(2,1)}, f32[48,2304]{1,0:T(8,128)}, f32[48,768]{1,0:T(8,128)}, f32[48,3072]{1,0:T(...) custom-call(bf16[512,768]{1,0:T(8,128)(2,1)} %bitcast.5, ...), custom_call_target="tpu_custom_call" | custom-call | tf_op jit(solution)/shard_map/pallas_call | solution.py:850
  118.8 4.3 %shard_map.255 = (bf16[512,768]{1,0:T(8,128)(2,1)}, bf16[512,768]{1,0:T(8,128)(2,1)}, f32[48]{0:T(128)}, f32[48]{0:T(128)}, f32[48,2304]{1,0:T(8,128)}, /*index=...) custom-call(bf16[512,768]{1,0:T(8,128)(2,1)} %get-tuple-element.37.o, ...), custom_call_target="tpu_custom_call" | custom-call | tf_op jit(solution)/shard_map/pallas_call | solution.py:887

commit v2 on v1

--- a/solution.py
+++ b/solution.py
@@ -8,7 +8,7 @@
 
 MESH = pl.DeviceIdType.MESH
 CHUNKS = 18
-LAG = 2
+AFTER = (2, 6, 10, 14, 18)
 RING = 9
 BF = jnp.bfloat16
 F32 = jnp.float32
@@ -21,31 +21,28 @@
         self.Y = blk
         self.dp = dp
         self.R = width // dp
-        self.ny = 2 if blk == 2 else 0
-        self.nx = 4 - self.ny
+        self.kinds = 2 if blk == 2 else 1
 
 
 def comm_scratch(g):
-    A, B, Y, R, nx, ny = g.A, g.B, g.Y, g.R, g.nx, g.ny
+    A, B, Y, R = g.A, g.B, g.Y, g.R
+    n = CHUNKS // g.kinds
     shapes = dict(
         r0=pltpu.VMEM((RING, 4, B, A, R, 128), BF),
-        rx=pltpu.VMEM((CHUNKS, B - 1, nx, A, R, 128), BF),
-        rz=pltpu.VMEM((CHUNKS, A - 1, nx, R, 128), BF),
-        ryx=pltpu.VMEM((CHUNKS, Y, nx, R, 128), BF),
+        rx=pltpu.VMEM((n, B - 1, 4, A, R, 128), BF),
+        rz=pltpu.VMEM((n, A - 1, 4, R, 128), BF),
+        ryx=pltpu.VMEM((n, Y, 4, R, 128), BF),
         s_core=pltpu.SemaphoreType.DMA((2, CHUNKS)),
         s_x=pltpu.SemaphoreType.DMA((2, CHUNKS, B - 1)),
-        s_z=pltpu.SemaphoreType.DMA((2, CHUNKS, A - 1)),
-        s_yx=pltpu.SemaphoreType.DMA((2, CHUNKS, Y - 1)),
+        s_z=pltpu.SemaphoreType.DMA((2, CHUNKS)),
+        s_y=pltpu.SemaphoreType.DMA((2, CHUNKS, Y - 1)),
     )
-    if ny:
+    if g.kinds == 2:
         shapes.update(
-            ry=pltpu.VMEM((CHUNKS, B, A, R, 128), BF),
-            rx2=pltpu.VMEM((CHUNKS, B - 1, A, R, 128), BF),
-            rz2=pltpu.VMEM((CHUNKS, A - 1, R, 128), BF),
-            rag=pltpu.VMEM((CHUNKS, 2, R, 128), BF),
-            s_y=pltpu.SemaphoreType.DMA((2, CHUNKS)),
-            s_x2=pltpu.SemaphoreType.DMA((2, CHUNKS, B - 1)),
-            s_z2=pltpu.SemaphoreType.DMA((2, CHUNKS, A - 1)),
+            ry=pltpu.VMEM((n, 2, B, A, R, 128), BF),
+            rx2=pltpu.VMEM((n, B - 1, 2, A, R, 128), BF),
+            rz2=pltpu.VMEM((n, A - 1, 2, R, 128), BF),
+            rag=pltpu.VMEM((n, 2, 2, R, 128), BF),
             s_ag=pltpu.SemaphoreType.DMA((2, CHUNKS)),
         )
     return shapes
@@ -94,165 +91,143 @@
             device_id_type=MESH,
         )
 
-    def stage0(self, j):
-        s = j % self.slots
-        return [self.copy(self.G.at[s, 1 - self.c], self.r0.at[j % RING], self.s_core, (j,), self.dev(c=1 - self.c))]
-
-    def stage1(self, j):
-        g, s = self.g, j % self.slots
-        out = []
+    def core(self, j, kind):
+        copy = self.copy(
+            self.G.at[j % self.slots, 1 - self.c], self.r0.at[j % RING], self.s_core, (j,), self.dev(c=1 - self.c)
+        )
+        return [copy], [copy]
+
+    def along_b(self, j, kind):
+        g, i = self.g, j // self.g.kinds
+        landing = self.rx2 if kind else self.rx
+        cols = pl.ds(2 * self.y, 2) if kind else pl.ds(0, 4)
+        copies = []
         for k in range(1, g.B):
             other = (self.b + k) % g.B
-            out.append(
-                self.copy(
-                    self.G.at[s, self.c, pl.ds(0, g.nx), other],
-                    self.rx.at[j, k - 1],
-                    self.s_x,
-                    (j, k - 1),
-                    self.dev(b=other),
-                )
-            )
-        if g.ny:
-            out.append(
-                self.copy(
-                    self.G.at[s, self.c, g.nx + 1 - self.y], self.ry.at[j], self.s_y, (j,), self.dev(y=1 - self.y)
-                )
-            )
-        return out
-
-    def stage2(self, j):
-        g, s = self.g, j % self.slots
-        out = []
+            source = self.G.at[j % self.slots, self.c, cols, other]
+            copies.append(self.copy(source, landing.at[i, k - 1], self.s_x, (j, k - 1), self.dev(b=other)))
+        return copies, copies
+
+    def along_a(self, j, kind):
+        g, i = self.g, j // self.g.kinds
+        landing = self.rz2 if kind else self.rz
+        cols = pl.ds(2 * self.y, 2) if kind else pl.ds(0, 4)
+        copies = []
         for k in range(1, g.A):
             other = (self.a + k) % g.A
-            out.append(
-                self.copy(
-                    self.G.at[s, self.c, pl.ds(0, g.nx), self.b, other],
-                    self.rz.at[j, k - 1],
-                    self.s_z,
-                    (j, k - 1),
-                    self.dev(a=other),
-                )
-            )
-        if g.ny:
-            for k in range(1, g.B):
-                other = (self.b + k) % g.B
-                out.append(
-                    self.copy(
-                        self.G.at[s, self.c, g.nx + self.y, other],
-                        self.rx2.at[j, k - 1],
-                        self.s_x2,
-                        (j, k - 1),
-                        self.dev(b=other),
-                    )
-                )
-        return out
-
-    def stage3(self, j):
-        g, s = self.g, j % self.slots
-        out = []
-        for k in range(1, g.Y):
-            other = (self.y + k) % g.Y
-            out.append(
-                self.copy(
-                    self.ryx.at[j, self.y], self.ryx.at[j, self.y], self.s_yx, (j, k - 1), self.dev(y=other)
-                )
-            )
-        if g.ny:
-            for k in range(1, g.A):
-                other = (self.a + k) % g.A
-                out.append(
-                    self.copy(
-                        self.G.at[s, self.c, g.nx + self.y, self.b, other],
-                        self.rz2.at[j, k - 1],
-                        self.s_z2,
-                        (j, k - 1),
-                        self.dev(a=other),
-                    )
-                )
-        return out
-
-    def stage4(self, j):
-        if not self.g.ny:
-            return []
-        return [self.copy(self.rag.at[j, self.y], self.rag.at[j, self.y], self.s_ag, (j,), self.dev(y=1 - self.y))]
-
-    def after0(self, j):
-        s = j % self.slots
-        g = self.g
-
-        def add(i, _):
-            col, b = i // g.B, i % g.B
-            mine = self.G.at[s, self.c, col, b]
-            mine[...] = mine[...] + self.r0[j % RING, col, b]
-            return 0
-
-        lax.fori_loop(0, 4 * g.B, add, 0)
-
-    def sum_into(self, mine, parts):
+            source = self.G.at[j % self.slots, self.c, cols, self.b, other]
+            copies.append(self.copy(source, landing.at[i, k - 1], self.s_z, (j,), self.dev(a=other)))
+        return copies, [self.copy(landing.at[i], landing.at[i], self.s_z, (j,), self.dev(a=(self.a + 1) % g.A))]
+
+    def along_blk(self, j, kind):
+        g, i = self.g, j // self.g.kinds
+        if kind:
+            source = self.G.at[j % self.slots, self.c, pl.ds(2 * (1 - self.y), 2)]
+            copies = [self.copy(source, self.ry.at[i], self.s_y, (j, 0), self.dev(y=1 - self.y))]
+            return copies, copies
+        mine = self.ryx.at[i, self.y]
+        copies = [
+            self.copy(mine, mine, self.s_y, (j, k - 1), self.dev(y=(self.y + k) % g.Y)) for k in range(1, g.Y)
+        ]
+        return copies, copies
+
+    def share(self, j, kind):
+        mine = self.rag.at[j // 2, self.y]
+        copies = [self.copy(mine, mine, self.s_ag, (j,), self.dev(y=1 - self.y))]
+        return copies, copies
+
+    def add(self, mine, parts):
+        if len(parts) == 1:
+            mine[...] = mine[...] + parts[0]
+        else:
+            mine[...] = self.summed(mine, parts)
+
+    def summed(self, mine, parts):
         total = mine[...].astype(F32)
         for part in parts:
             total = total + part.astype(F32)
-        mine[...] = total.astype(BF)
-
-    def after1(self, j):
-        g, s = self.g, j % self.slots
-        for col in range(g.nx):
-            self.sum_into(
-                self.G.at[s, self.c, col, self.b], [self.rx[j, k, col] for k in range(g.B - 1)]
-            )
-        if g.ny:
-            for b in range(g.B):
-                self.sum_into(self.G.at[s, self.c, g.nx + self.y, b], [self.ry[j, b]])
-
-    def after2(self, j):
-        g, s = self.g, j % self.slots
-        total = self.G[s, self.c, pl.ds(0, g.nx), self.b, self.a].astype(F32)
-        for k in range(g.A - 1):
-            total = total + self.rz[j, k].astype(F32)
-        self.ryx[j, self.y] = total.astype(BF)
-        if g.ny:
-            self.sum_into(
-                self.G.at[s, self.c, g.nx + self.y, self.b], [self.rx2[j, k] for k in range(g.B - 1)]
-            )
-
-    def after3(self, j):
-        g, s = self.g, j % self.slots
-        total = self.ryx[j, 0].astype(F32)
+        return total.astype(BF)
+
+    def after_core(self, j, kind):
+        self.add(self.G.at[j % self.slots, self.c], [self.r0[j % RING]])
+
+    def after_b(self, j, kind):
+        g, i = self.g, j // self.g.kinds
+        landing = self.rx2 if kind else self.rx
+        cols = pl.ds(2 * self.y, 2) if kind else pl.ds(0, 4)
+        self.add(self.G.at[j % self.slots, self.c, cols, self.b], [landing[i, k] for k in range(g.B - 1)])
+
+    def after_a(self, j, kind):
+        g, i = self.g, j // self.g.kinds
+        landing = self.rz2 if kind else self.rz
+        cols = pl.ds(2 * self.y, 2) if kind else pl.ds(0, 4)
+        total = self.summed(
+            self.G.at[j % self.slots, self.c, cols, self.b, self.a], [landing[i, k] for k in range(g.A - 1)]
+        )
+        if kind:
+            self.rag[i, self.y] = total
+        else:
+            self.ryx[i, self.y] = total
+
+    def after_blk(self, j, kind):
+        g, i = self.g, j // self.g.kinds
+        if kind:
+            self.add(self.G.at[j % self.slots, self.c, pl.ds(2 * self.y, 2)], [self.ry[i]])
+            return
+        total = self.ryx[i, 0].astype(F32)
         for k in range(1, g.Y):
-            total = total + self.ryx[j, k].astype(F32)
-        for col in range(g.nx):
-            self.emit(j, col, total[col])
-        if g.ny:
-            total = self.G[s, self.c, g.nx + self.y, self.b, self.a].astype(F32)
-            for k in range(g.A - 1):
-                total = total + self.rz2[j, k].astype(F32)
-            self.rag[j, self.y] = total.astype(BF)
-
-    def after4(self, j):
-        for k in range(self.g.ny):
-            self.emit(j, self.g.nx + k, self.rag[j, k].astype(F32))
-
-    def start(self, stage, j):
-        for copy in (self.stage0, self.stage1, self.stage2, self.stage3, self.stage4)[stage](j):
-            copy.start()
+            total = total + self.ryx[i, k].astype(F32)
+        self.emit(j, [total[col] for col in range(4)])
+
+    def after_share(self, j, kind):
+        i = j // 2
+        self.emit(j, [self.rag[i, col // 2, col % 2].astype(F32) for col in range(4)])
+
+    def plan(self, kind):
+        core = (self.core, self.after_core)
+        b = (self.along_b, self.after_b)
+        a = (self.along_a, self.after_a)
+        blk = (self.along_blk, self.after_blk)
+        share = (self.share, self.after_share)
+        return (core, blk, b, a, share) if kind else (core, b, a, blk)
+
+    def start(self, j):
+        self.core(j, 0)[0][0].start()
 
     def finish(self, stage, j):
-        for copy in (self.stage0, self.stage1, self.stage2, self.stage3, self.stage4)[stage](j):
-            copy.wait()
-        (self.after0, self.after1, self.after2, self.after3, self.after4)[stage](j)
-        if stage < 4:
-            self.start(stage + 1, j)
-
-    def advance(self, t, first=0, last=CHUNKS):
-        for stage in range(4, -1, -1):
-            j = t - LAG * stage
-            if isinstance(j, int):
-                if first <= j < last:
-                    self.finish(stage, j)
+        for kind in range(self.g.kinds):
+            plan = self.plan(kind)
+            if stage >= len(plan):
+                continue
+
+            def go(kind=kind, plan=plan):
+                for copy in plan[stage][0](j, kind)[1]:
+                    copy.wait()
+                plan[stage][1](j, kind)
+                if stage + 1 < len(plan):
+                    for copy in plan[stage + 1][0](j, kind)[0]:
+                        copy.start()
+
+            if self.g.kinds == 1:
+                go()
+            elif isinstance(j, int):
+                if j % 2 == kind:
+                    go()
             else:
-
-                @pl.when((j >= first) & (j < last))
+                pl.when(j % 2 == kind)(go)
+
+    def advance(self, t):
+        for stage in range(5):
+            twice = t - AFTER[stage]
+            if twice % 2 == 0 and 0 <= twice < 2 * CHUNKS:
+                self.finish(stage, twice // 2)
+
+    def advance_two(self, t, odd):
+        for stage in range(5):
+            if (odd - AFTER[stage]) % 2 == 0:
+                j = t + (odd - AFTER[stage]) // 2
+
+                @pl.when((j >= 0) & (j < CHUNKS))
                 def _(stage=stage, j=j):
                     self.finish(stage, j)
 
@@ -260,22 +235,23 @@
 def emit_to(g, j_ref, o_ref, e_ref, r_ref):
     R = g.R
 
-    def emit(j, col, value):
+    def emit(j, values):
         @pl.when(j < 6)
         def _():
-            e_ref[:, pl.ds(pl.multiple_of(j * 512 + col * 128, 128), 128)] = value
+            for col in range(4):
+                e_ref[:, pl.ds(pl.multiple_of(j * 512 + col * 128, 128), 128)] = values[col]
 
         @pl.when((j >= 6) & (j < 12))
         def _():
-            r_ref[pl.ds(col * R, R), pl.ds(pl.multiple_of((j - 6) * 128, 128), 128)] = value
+            for k in range(4):
+                r_ref[k * R : (k + 1) * R, pl.ds(pl.multiple_of((j - 6) * 128, 128), 128)] = values[k]
 
         @pl.when(j >= 12)
         def _():
             at = pl.multiple_of((j - 12) * 128, 128)
-            if col < 3:
-                j_ref[:, pl.ds(pl.multiple_of(col * 768 + at, 128), 128)] = value
-            else:
-                o_ref[:, pl.ds(at, 128)] = value
+            for k in range(3):
+                j_ref[:, pl.ds(pl.multiple_of(k * 768 + at, 128), 128)] = values[k]
+            o_ref[:, pl.ds(at, 128)] = values[3]
 
     return emit
 
@@ -292,6 +268,7 @@
 EDGE = 128
 SPAN = 3 * EDGE
 PAIRS = HEADS // 2
+NEAR = 112
 SLOTS = 12
 STREAM = 2
 TICK = 512
@@ -467,19 +444,35 @@
 
     top = lax.broadcasted_iota(jnp.int32, (EDGE, 1), 0) < HD
 
+    def scores_of(p, b):
+        at = pl.ds(pl.multiple_of(p * 128, 128), 128)
+        keys, own = pl.ds(b * EDGE, SPAN), pl.ds(b * EDGE, EDGE)
+        both = jnp.concatenate([r["qe"][own, at], r["qo"][own, at]], axis=0)
+        return nt(r["k"][keys, at], both)
+
+    def probs_of(b, scores):
+        bias = r["bias"][b]
+        scores = scores + jnp.concatenate([bias, bias], axis=1)
+        powers = jnp.exp(scores - jnp.max(scores, axis=0, keepdims=True))
+        return (powers * (1.0 / column_sum(powers))).astype(BF)
+
+    def mix(p, b, probs):
+        at = pl.ds(pl.multiple_of(p * 128, 128), 128)
+        keys, own = pl.ds(b * EDGE, SPAN), pl.ds(b * EDGE, EDGE)
+        r["probs"][p, b] = probs
+        mixed = nn(r["vT"][at, keys], probs)
+        r["attT"][at, own] = jnp.where(top, mixed[:, :128], mixed[:, 128:]).astype(BF)
+
     def attend(p, _):
-        at = pl.ds(pl.multiple_of(p * 128, 128), 128)
+        scores = scores_of(p, 0)
+        before = None
         for b in range(4):
-            keys, own = pl.ds(b * EDGE, SPAN), pl.ds(b * EDGE, EDGE)
-            both = jnp.concatenate([r["qe"][own, at], r["qo"][own, at]], axis=0)
-            scores = nt(r["k"][keys, at], both)
-            bias = r["bias"][b]
-            scores = scores + jnp.concatenate([bias, bias], axis=1)
-            powers = jnp.exp(scores - jnp.max(scores, axis=0, keepdims=True))
-            probs = (powers * (1.0 / column_sum(powers))).astype(BF)
-            r["probs"][p, b] = probs
-            mixed = nn(r["vT"][at, keys], probs)
-            r["attT"][at, own] = jnp.where(top, mixed[:, :128], mixed[:, 128:]).astype(BF)
+            following = scores_of(p, b + 1) if b < 3 else None
+            probs = probs_of(b, scores)
+            if b > 0:
+                mix(p, b - 1, before)
+            before, scores = probs, following
+        mix(p, 3, before)
         return 0
 
     lax.fori_loop(0, PAIRS, attend, 0)
@@ -512,31 +505,33 @@
         at = pl.ds(pl.multiple_of(i * TICK, TICK), TICK)
         bias = r["expand_bias"][:, at]
         bias_sum = jnp.zeros((1, TICK), F32)
-        for half in range(2):
-            rows = pl.ds(half * 256, 256)
-            hidden = nn(n2[rows, :], we[...]) + bias
-            back = nt(dy[rows, :], wr[...])
-            share, slope = normal_parts(hidden)
-            active = (hidden * share).astype(BF)
-            hidden_gradient = back * (share + slope)
+        rows = [pl.ds(half * 256, 256) for half in range(2)]
+        hidden = [nn(n2[part, :], we[...]) + bias for part in rows]
+        back = [nt(dy[part, :], wr[...]) for part in rows]
+        for half, part in enumerate(rows):
+            share, slope = normal_parts(hidden[half])
+            active = (hidden[half] * share).astype(BF)
+            hidden_gradient = back[half] * (share + slope)
             bias_sum = bias_sum + column_sum(hidden_gradient)
             low = hidden_gradient.astype(BF)
-            r["hl"][rows, :] = low
-            r["actT"][at, rows] = active.T
-            total[rows, :] += nn(active, wr[...])
-            r["dn"][rows, :] += nt(low, we[...])
+            r["hl"][part, :] = low
+            r["actT"][at, part] = active.T
+            total[part, :] += nn(active, wr[...])
+            r["dn"][part, :] += nt(low, we[...])
+            if half == 0:
+                comm.advance_two(i, -1)
         r["eb"][:, at] = bias_sum
         for part in range(2):
             block = nn(n2T[part * 384 : (part + 1) * 384, :], r["hl"][...]).astype(BF)
             store_rows(block, i, part * 2, 2)
-        comm.start(0, i)
+        comm.start(i)
 
         @pl.when(i + STREAM < TICKS)
         def _():
             for copy in ffn_loads(i + STREAM):
                 copy.start()
 
-        comm.advance(i - 1)
+        comm.advance_two(i, 0)
         return 0
 
     def store_rows(block, chunk, a0, na):
@@ -566,9 +561,10 @@
             return 0
 
         lax.fori_loop(0, A, part, 0)
-        comm.start(0, chunk)
-        comm.start(0, chunk + 1)
-        comm.advance(5 + p)
+        comm.start(chunk)
+        comm.start(chunk + 1)
+        comm.advance_two(6 + p, -1)
+        comm.advance_two(6 + p, 0)
         return 0
 
     lax.fori_loop(0, 3, reduce_gradient, 0)
@@ -604,7 +600,8 @@
     save_out.start()
     for k in range(4):
         vec[7 + k : 8 + k, :] = r["eb"][:, k * D : (k + 1) * D]
-    comm.advance(8)
+    comm.advance(17)
+    comm.advance(18)
 
     parts, jq, sent, got, s_part = r["parts"], r["jq"], r["sent"], r["got"], r["s_part"]
 
@@ -619,33 +616,49 @@
         slot = p % 2
         own_sum = jnp.zeros((1, 128), F32)
         parts[slot] = jnp.zeros((ROWS + 2 * EDGE, 256), F32)
-        for b in range(4):
+
+        def errors_of(b):
+            own = pl.ds(b * EDGE, EDGE)
+            return jnp.concatenate([r["oe"][own, at], r["oo"][own, at]], axis=0)
+
+        def shares_of(b):
+            return nt(r["v"][pl.ds(b * EDGE, SPAN), at], errors_of(b))
+
+        def score_gradient_of(b, shares):
+            wide = r["probs"][p, b].astype(F32)
+            product = wide * shares
+            return (product - wide * column_sum(product)).astype(BF)
+
+        def spread(b, low):
             keys, own = pl.ds(b * EDGE, SPAN), pl.ds(b * EDGE, EDGE)
             queries = jnp.concatenate([r["qe"][own, at], r["qo"][own, at]], axis=0)
-            errors = jnp.concatenate([r["oe"][own, at], r["oo"][own, at]], axis=0)
-            shares = nt(r["v"][keys, at], errors)
-            probs = r["probs"][p, b]
-            wide = probs.astype(F32)
-            product = wide * shares
-            delta = column_sum(product)
-            low = (product - wide * delta).astype(BF)
             parts[slot, keys, 0:128] += nn(low, queries)
-            parts[slot, keys, 128:256] += nn(probs, errors)
+            parts[slot, keys, 128:256] += nn(r["probs"][p, b], errors_of(b))
             turned = nn(r["kT"][at, keys], low)
             mine = (jnp.where(top, turned[:, :128], turned[:, 128:]) * HD**-0.5).T
-            own_sum = own_sum + column_sum(mine)
             jq[slot, own, :] = mine.astype(BF)
+            return column_sum(mine)
+
+        shares = shares_of(0)
+        before = None
+        for b in range(4):
+            following = shares_of(b + 1) if b < 3 else None
+            low = score_gradient_of(b, shares)
+            if b > 0:
+                own_sum = own_sum + spread(b - 1, before)
+            before, shares = low, following
+        own_sum = own_sum + spread(3, before)
         vec[2:3, at] = own_sum
         to_left, to_right = part_copies(p)
 
         @pl.when(has_left)
         def _():
-            sent[slot, 0] = parts[slot, 0:EDGE, :].astype(BF)
+            sent[slot, 0] = parts[slot, EDGE - NEAR : EDGE, :].astype(BF)
             to_left.start()
 
         @pl.when(has_right)
         def _():
-            sent[slot, 1] = parts[slot, ROWS + EDGE :, :].astype(BF)
+            sent[slot, 1] = parts[slot, ROWS + EDGE : ROWS + EDGE + NEAR, :].astype(BF)
             to_right.start()
 
     def joint_gradient(p):
@@ -657,13 +670,13 @@
         def _():
             to_left.wait_send()
             to_right.wait_recv()
-            parts[slot, EDGE : 2 * EDGE, :] += got[p, 0].astype(F32)
+            parts[slot, EDGE : EDGE + NEAR, :] += got[p, 0].astype(F32)
 
         @pl.when(has_right)
         def _():
             to_right.wait_send()
             to_left.wait_recv()
-            parts[slot, ROWS : ROWS + EDGE, :] += got[p, 1].astype(F32)
+            parts[slot, ROWS + EDGE - NEAR : ROWS + EDGE, :] += got[p, 1].astype(F32)
 
         sums = parts[slot, EDGE : ROWS + EDGE, :]
         vec[3:4, at] = column_sum(sums[:, 128:])
@@ -677,18 +690,20 @@
             block = nn(r["n1T"][rows, :], low).astype(BF)
             block_out = nn(r["attT"][rows, :], low_out).astype(BF)
             store_rows(jnp.concatenate([block, block_out], axis=1), 12 + p, part * 2, 2)
-        comm.start(0, 12 + p)
+        comm.start(12 + p)
 
     def pair_step(i, _):
         @pl.when(i < PAIRS)
         def _():
             attend_back(i)
 
+        comm.advance_two(9 + i, 1)
+
         @pl.when(i > 0)
         def _():
             joint_gradient(i - 1)
 
-        comm.advance(9 + i)
+        comm.advance_two(10 + i, 0)
         return 0
 
     lax.fori_loop(0, PAIRS + 1, pair_step, 0)
@@ -749,7 +764,8 @@
 
     vector_start(0, vec[...])
     for step in range(4):
-        comm.advance(16 + step)
+        comm.advance(33 + 2 * step)
+        comm.advance(34 + 2 * step)
         vector_wait(step)
         if step < 3:
             vector_start(step + 1, vector_sum(step))
@@ -769,7 +785,7 @@
     r["v_out"][...] = picked[:, 0:128]
     r["jb_out"][...] = column_sum(jnp.where(kind == 2 + place // n2v, picked[:, 128:256], 0.0))
     r["eb_out"][...] = column_sum(jnp.where(kind == 7 + place // n4v, picked[:, 256:512], 0.0))
-    for t in range(20, CHUNKS + 4 * LAG):
+    for t in range(41, 2 * CHUNKS + AFTER[4]):
         comm.advance(t)
     save_out.wait()
     save_dx.wait()
@@ -831,8 +847,8 @@
         ml=pltpu.VMEM((ROWS, D), BF),
         parts=pltpu.VMEM((2, ext, 256), F32),
         jq=pltpu.VMEM((2, ROWS, 128), BF),
-        sent=pltpu.VMEM((2, 2, EDGE, 256), BF),
-        got=pltpu.VMEM((PAIRS, 2, EDGE, 256), BF),
+        sent=pltpu.VMEM((2, 2, NEAR, 256), BF),
+        got=pltpu.VMEM((PAIRS, 2, NEAR, 256), BF),
         vec=pltpu.VMEM((16, D), F32),
         rv=pltpu.VMEM((2 + B, 16, D), F32),
         rvl=pltpu.VMEM((A + Y, 16, D), BF),

time: 123 us -> 113 us (0.919)
  Pallas kernels: 122 us -> 112 us
    pallas_call x1, Pallas kernels: 118 us -> 108 us  [layer(): pl.pallas_call(functools.partial(layer_kernel, g, names), out_shape=tuple...]
where the time goes in v2:
time: 113 us
  Pallas kernels  112 us (99%)
    pallas_call x1, Pallas kernels, layer(): pl.pallas_call(functools.partial(layer_kernel, g, names), out_shape=tuple...  108 us
    pallas_call x1, Pallas kernels, hand_over(): pl.pallas_call(functools.partial(hand_over_kernel, g), out_shape=tuple((j...  4.28 us

profile of v2, /device:TPU:0, one launch (start us, length us, event | category | flops | bytes accessed | tf_op | source)
XLA Modules:
  0.0 112.6 jit_solution(12355502883975011900)
XLA Ops:
  0.7 107.7 %shard_map.254 = (bf16[512,768]{1,0:T(8,128)(2,1)}, bf16[512,768]{1,0:T(8,128)(2,1)}, f32[48,2304]{1,0:T(8,128)}, f32[48,768]{1,0:T(8,128)}, f32[48,3072]{1,0:T(...) custom-call(bf16[512,768]{1,0:T(8,128)(2,1)} %bitcast.5, ...), custom_call_target="tpu_custom_call" | custom-call | tf_op jit(solution)/shard_map/pallas_call | solution.py:866
  108.3 4.3 %shard_map.255 = (bf16[512,768]{1,0:T(8,128)(2,1)}, bf16[512,768]{1,0:T(8,128)(2,1)}, f32[48]{0:T(128)}, f32[48]{0:T(128)}, f32[48,2304]{1,0:T(8,128)}, /*index=...) custom-call(bf16[512,768]{1,0:T(8,128)(2,1)} %get-tuple-element.37.o, ...), custom_call_target="tpu_custom_call" | custom-call | tf_op jit(solution)/shard_map/pallas_call | solution.py:903

commit v3 on v2

--- a/solution.py
+++ b/solution.py
@@ -211,10 +211,10 @@
             if self.g.kinds == 1:
                 go()
             elif isinstance(j, int):
-                if j % 2 == kind:
+                if (j + (j >= CHUNKS - 2)) % 2 == kind:
                     go()
             else:
-                pl.when(j % 2 == kind)(go)
+                pl.when(jnp.where(j >= CHUNKS - 2, j + 1, j) % 2 == kind)(go)
 
     def advance(self, t):
         for stage in range(5):
@@ -401,12 +401,11 @@
         wj = r["wj"]
         key_rows = nn(low, wj[:, D : 2 * D]).astype(BF)
         r["k"][pl.ds(at, count), :] = key_rows
-        r["kT"][:, pl.ds(at, count)] = key_rows.T
         value_rows = (nn(low, wj[:, 2 * D :]) + r["joint_bias"][:, D:]).astype(BF)
         r["v"][pl.ds(at, count), :] = value_rows
         r["vT"][:, pl.ds(at, count)] = value_rows.T
         if own:
-            r["n1T"][:, pl.ds(row_at, count)] = low.T
+            r["ml"][pl.ds(row_at, count), :] = low
             queries = (nn(low, wj[:, :D]) + r["joint_bias"][:, :D]).astype(BF) * BF(HD**-0.5)
             r["qe"][pl.ds(row_at, count), :] = jnp.where(even, queries, BF(0))
             r["qo"][pl.ds(row_at, count), :] = jnp.where(even, BF(0), queries)
@@ -545,6 +544,18 @@
 
     lax.fori_loop(0, TICKS, feed_forward, 0)
 
+    def turn(i, _):
+        at = pl.ds(pl.multiple_of(i * 256, 256), 256)
+        r["kT"][:, at] = r["k"][at, :].T
+
+        @pl.when(i < 2)
+        def _():
+            r["n1T"][:, at] = r["ml"][at, :].T
+
+        return 0
+
+    lax.fori_loop(0, 3, turn, 0)
+
     def reduce_gradient(p, _):
         at = pl.ds(pl.multiple_of(p * 256, 256), 256)
         chunk = 6 + 2 * p
@@ -696,8 +707,6 @@
         @pl.when(i < PAIRS)
         def _():
             attend_back(i)
-
-        comm.advance_two(9 + i, 1)
 
         @pl.when(i > 0)
         def _():
@@ -877,11 +886,15 @@
 
 
 def hand_over_kernel(g, out, dx, j, o, e, w, v, jb, eb, *refs):
-    outs, sems = refs[:14], refs[14]
+    outs, held, sems = refs[:14], refs[14:20], refs[20]
     R = g.R
     moves = [(out, 0), (dx, 1), (j, 4), (o, 6), (e, 10), (w, 12)]
-    copies = [pltpu.make_async_copy(src, outs[k], sems.at[i]) for i, (src, k) in enumerate(moves)]
-    for copy in copies:
+    loads = [pltpu.make_async_copy(src, held[i], sems.at[0, i]) for i, (src, _) in enumerate(moves)]
+    copies = [pltpu.make_async_copy(held[i], outs[k], sems.at[1, i]) for i, (_, k) in enumerate(moves)]
+    for load in loads:
+        load.start()
+    for load, copy in zip(loads, copies):
+        load.wait()
         copy.start()
     for row, k in ((0, 2), (1, 3), (4, 7), (5, 8), (6, 9), (11, 13)):
         outs[k][...] = v[row, :R]
@@ -903,9 +916,12 @@
     return pl.pallas_call(
         functools.partial(hand_over_kernel, g),
         out_shape=tuple(jax.ShapeDtypeStruct(*shape) for shape in shapes),
-        in_specs=[V] * 9,
+        in_specs=[H] * 6 + [V] * 3,
         out_specs=[V if len(shape) == 1 else H for shape, _ in shapes],
-        scratch_shapes=[pltpu.SemaphoreType.DMA((6,))],
+        scratch_shapes=[
+            *(pltpu.VMEM(o[name].shape, o[name].dtype) for name in names[:6]),
+            pltpu.SemaphoreType.DMA((2, 6)),
+        ],
     )(*(o[name] for name in names))
 
 

time: 113 us -> 111 us (0.982)
  Pallas kernels: 112 us -> 110 us
    pallas_call x1, Pallas kernels: 108 us -> 106 us  [layer(): pl.pallas_call(functools.partial(layer_kernel, g, names), out_shape=tuple...]
where the time goes in v3:
time: 111 us
  Pallas kernels  110 us (99%)
    pallas_call x1, Pallas kernels, layer(): pl.pallas_call(functools.partial(layer_kernel, g, names), out_shape=tuple...  106 us
    pallas_call x1, Pallas kernels, hand_over(): pl.pallas_call(functools.partial(hand_over_kernel, g), out_shape=tuple((j...  4.26 us

profile of v3, /device:TPU:0, one launch (start us, length us, event | category | flops | bytes accessed | tf_op | source)
XLA Modules:
  0.0 110.8 jit_solution(5959650996964562982)
XLA Ops:
  0.7 105.9 %shard_map.254 = (bf16[512,768]{1,0:T(8,128)(2,1)}, bf16[512,768]{1,0:T(8,128)(2,1)}, f32[48,2304]{1,0:T(8,128)}, f32[48,768]{1,0:T(8,128)}, f32[48,3072]{1,0:T(...) custom-call(bf16[512,768]{1,0:T(8,128)(2,1)} %bitcast.5, ...), custom_call_target="tpu_custom_call" | custom-call | tf_op jit(solution)/shard_map/pallas_call | solution.py:875
  106.5 4.3 %shard_map.255 = (bf16[512,768]{1,0:T(8,128)(2,1)}, bf16[512,768]{1,0:T(8,128)(2,1)}, f32[48]{0:T(128)}, f32[48]{0:T(128)}, f32[48,2304]{1,0:T(8,128)}, /*index=...) custom-call(bf16[512,768]{1,0:T(8,128)(2,1)} %get-tuple-element.37.o, ...), custom_call_target="tpu_custom_call" | custom-call | tf_op jit(solution)/shard_map/pallas_call | solution.py:916

commit v4 on v3

--- a/solution.py
+++ b/solution.py
@@ -10,6 +10,7 @@
 CHUNKS = 18
 AFTER = (2, 6, 10, 14, 18)
 RING = 9
+VECTOR_STEPS = (36, 40, 44, 48)
 BF = jnp.bfloat16
 F32 = jnp.float32
 
@@ -319,7 +320,7 @@
     r["oe"], r["oo"] = r["vT"], r["n2"]
     out_rows, dx_rows = r["k"].at[pl.ds(0, ROWS)], r["ml"]
     x, xh, dy = r["x"], r["xh"], r["dy"]
-    comm = Comm(g, G, SLOTS, r, emit_to(g, r["j_out"], r["o_out"], r["e_out"], r["r_out"]))
+    comm = Comm(g, G, SLOTS, r, emit_to(g, r["j_out"], r["o_out"], r["e_sum"], r["r_sum"]))
     y = comm.y
     has_left, has_right = y > 0, y < Y - 1
 
@@ -517,8 +518,6 @@
             r["actT"][at, part] = active.T
             total[part, :] += nn(active, wr[...])
             r["dn"][part, :] += nt(low, we[...])
-            if half == 0:
-                comm.advance_two(i, -1)
         r["eb"][:, at] = bias_sum
         for part in range(2):
             block = nn(n2T[part * 384 : (part + 1) * 384, :], r["hl"][...]).astype(BF)
@@ -574,7 +573,6 @@
         lax.fori_loop(0, A, part, 0)
         comm.start(chunk)
         comm.start(chunk + 1)
-        comm.advance_two(6 + p, -1)
         comm.advance_two(6 + p, 0)
         return 0
 
@@ -614,6 +612,17 @@
     comm.advance(17)
     comm.advance(18)
 
+    place = lax.axis_index("dp")
+    n2v, n4v = g.dp // 2, g.dp // 4
+    lane = lax.broadcasted_iota(jnp.int32, (1, ROWS), 1)
+    want = jnp.where(
+        lane < 128,
+        lane + place * R,
+        jnp.where(lane < 256, lane - 128 + (place % n2v) * (2 * R), lane - 256 + (place % n4v) * (4 * R)),
+    )
+    spot = lax.broadcasted_iota(jnp.int32, (D, ROWS), 0)
+    r["n2T"][...] = jnp.where(spot == want, 1.0, 0.0).astype(BF)
+
     parts, jq, sent, got, s_part = r["parts"], r["jq"], r["sent"], r["got"], r["s_part"]
 
     def part_copies(p):
@@ -650,27 +659,32 @@
             jq[slot, own, :] = mine.astype(BF)
             return column_sum(mine)
 
-        shares = shares_of(0)
+        to_left, to_right = part_copies(p)
+
+        def send_edges():
+            @pl.when(has_left)
+            def _():
+                sent[slot, 0] = parts[slot, EDGE - NEAR : EDGE, :].astype(BF)
+                to_left.start()
+
+            @pl.when(has_right)
+            def _():
+                sent[slot, 1] = parts[slot, ROWS + EDGE : ROWS + EDGE + NEAR, :].astype(BF)
+                to_right.start()
+
+        order = (0, 3, 1, 2)
+        shares = shares_of(order[0])
         before = None
-        for b in range(4):
-            following = shares_of(b + 1) if b < 3 else None
+        for step, b in enumerate(order):
+            following = shares_of(order[step + 1]) if step < 3 else None
             low = score_gradient_of(b, shares)
-            if b > 0:
-                own_sum = own_sum + spread(b - 1, before)
+            if step > 0:
+                own_sum = own_sum + spread(order[step - 1], before)
+            if step == 2:
+                send_edges()
             before, shares = low, following
-        own_sum = own_sum + spread(3, before)
+        own_sum = own_sum + spread(order[3], before)
         vec[2:3, at] = own_sum
-        to_left, to_right = part_copies(p)
-
-        @pl.when(has_left)
-        def _():
-            sent[slot, 0] = parts[slot, EDGE - NEAR : EDGE, :].astype(BF)
-            to_left.start()
-
-        @pl.when(has_right)
-        def _():
-            sent[slot, 1] = parts[slot, ROWS + EDGE : ROWS + EDGE + NEAR, :].astype(BF)
-            to_right.start()
 
     def joint_gradient(p):
         at = pl.ds(pl.multiple_of(p * 128, 128), 128)
@@ -771,31 +785,33 @@
         for copy in vector_copies(step)[1]:
             copy.wait()
 
+    def pick_vectors():
+        summed = vector_sum(3)
+        high = summed.astype(BF)
+        rest = (summed - high.astype(F32)).astype(BF)
+        picked = nn(high, r["n2T"][...]) + nn(rest, r["n2T"][...])
+        kind = lax.broadcasted_iota(jnp.int32, (16, 1), 0)
+        r["v_out"][...] = picked[:, 0:128]
+        r["jb_out"][...] = column_sum(jnp.where(kind == 2 + place // n2v, picked[:, 128:256], 0.0))
+        r["eb_out"][...] = column_sum(jnp.where(kind == 7 + place // n4v, picked[:, 256:512], 0.0))
+
+    save_e = pltpu.make_async_copy(r["e_sum"], r["e_out"], r["save"].at[2])
+    save_r = pltpu.make_async_copy(r["r_sum"], r["r_out"], r["save"].at[3])
     vector_start(0, vec[...])
-    for step in range(4):
-        comm.advance(33 + 2 * step)
-        comm.advance(34 + 2 * step)
-        vector_wait(step)
-        if step < 3:
-            vector_start(step + 1, vector_sum(step))
-    summed = vector_sum(3)
-    place = lax.axis_index("dp")
-    spot = lax.broadcasted_iota(jnp.int32, (D, 512), 0)
-    lane = lax.broadcasted_iota(jnp.int32, (D, 512), 1)
-    n2v, n4v = g.dp // 2, g.dp // 4
-    want = jnp.where(
-        lane < 128,
-        lane + place * R,
-        jnp.where(lane < 256, lane - 128 + (place % n2v) * (2 * R), lane - 256 + (place % n4v) * (4 * R)),
-    )
-    pick = jnp.where(spot == want, 1.0, 0.0).astype(F32)
-    picked = jnp.dot(summed, pick, precision=lax.Precision.HIGHEST, preferred_element_type=F32)
-    kind = lax.broadcasted_iota(jnp.int32, (16, 1), 0)
-    r["v_out"][...] = picked[:, 0:128]
-    r["jb_out"][...] = column_sum(jnp.where(kind == 2 + place // n2v, picked[:, 128:256], 0.0))
-    r["eb_out"][...] = column_sum(jnp.where(kind == 7 + place // n4v, picked[:, 256:512], 0.0))
-    for t in range(41, 2 * CHUNKS + AFTER[4]):
+    for t in range(34, 2 * CHUNKS + AFTER[4] - 1, 2):
         comm.advance(t)
+        if t in VECTOR_STEPS:
+            step = VECTOR_STEPS.index(t)
+            vector_wait(step)
+            if step < 3:
+                vector_start(step + 1, vector_sum(step))
+            else:
+                pick_vectors()
+        if t == 2 * 11 + AFTER[4]:
+            save_e.start()
+            save_r.start()
+    save_e.wait()
+    save_r.wait()
     save_out.wait()
     save_dx.wait()
 
@@ -863,7 +879,9 @@
         rvl=pltpu.VMEM((A + Y, 16, D), BF),
         G=pltpu.VMEM((SLOTS, 2, 4, B, A, R, 128), BF),
         load=pltpu.SemaphoreType.DMA((4,)),
-        save=pltpu.SemaphoreType.DMA((2,)),
+        save=pltpu.SemaphoreType.DMA((4,)),
+        e_sum=pltpu.VMEM((R, FF), F32),
+        r_sum=pltpu.VMEM((4 * R, D), F32),
         stream=pltpu.SemaphoreType.DMA((2, STREAM)),
         s_edge=pltpu.SemaphoreType.DMA((2, 2)),
         s_part=pltpu.SemaphoreType.DMA((2, PAIRS, 2)),
@@ -876,7 +894,7 @@
         functools.partial(layer_kernel, g, names),
         out_shape=tuple(jax.ShapeDtypeStruct(*shape) for shape in outputs.values()),
         in_specs=[spec for _, spec in inputs.values()],
-        out_specs=[H, H] + [V] * (len(outputs) - 2),
+        out_specs=[H if name in ("out", "dx", "e_out", "r_out") else V for name in outputs],
         scratch_shapes=list(scratch.values()),
         compiler_params=pltpu.CompilerParams(
             collective_id=0, has_side_effects=True, vmem_limit_bytes=64 << 20

time: 111 us -> 111 us (level)
  no operation moved by 1% of the time
where the time goes in v4:
time: 111 us; the launch traced here: 110 us
  Pallas kernels  110 us (99%)
    pallas_call x1, Pallas kernels, layer(): pl.pallas_call(functools.partial(layer_kernel, g, names), out_shape=tuple...  105 us
    pallas_call x1, Pallas kernels, hand_over(): pl.pallas_call(functools.partial(hand_over_kernel, g), out_shape=tuple((j...  4.26 us

profile of v4, /device:TPU:0, one launch (start us, length us, event | category | flops | bytes accessed | tf_op | source)
XLA Modules:
  0.0 110.2 jit_solution(12462290967252712127)
XLA Ops:
  0.7 105.3 %shard_map.254 = (bf16[512,768]{1,0:T(8,128)(2,1)}, bf16[512,768]{1,0:T(8,128)(2,1)}, f32[48,2304]{1,0:T(8,128)}, f32[48,768]{1,0:T(8,128)}, f32[48,3072]{1,0:T(...) custom-call(bf16[512,768]{1,0:T(8,128)(2,1)} %bitcast.5, ...), custom_call_target="tpu_custom_call" | custom-call | tf_op jit(solution)/shard_map/pallas_call | solution.py:893
  106.0 4.3 %shard_map.255 = (bf16[512,768]{1,0:T(8,128)(2,1)}, bf16[512,768]{1,0:T(8,128)(2,1)}, f32[48]{0:T(128)}, f32[48]{0:T(128)}, f32[48,2304]{1,0:T(8,128)}, /*index=...) custom-call(bf16[512,768]{1,0:T(8,128)(2,1)} %get-tuple-element.37.o, ...), custom_call_target="tpu_custom_call" | custom-call | tf_op jit(solution)/shard_map/pallas_call | solution.py:934

commit v5 on v4

--- a/solution.py
+++ b/solution.py
@@ -353,8 +353,8 @@
 
     def x_edges():
         return (
-            edge((), 0, patches.at[pl.ds(0, EDGE)], xh.at[1], r["s_edge"]),
-            edge((), 1, patches.at[pl.ds(ROWS - EDGE, EDGE)], xh.at[0], r["s_edge"]),
+            edge((), 0, patches.at[pl.ds(0, NEAR)], xh.at[1, pl.ds(0, NEAR)], r["s_edge"]),
+            edge((), 1, patches.at[pl.ds(ROWS - NEAR, NEAR)], xh.at[0, pl.ds(EDGE - NEAR, NEAR)], r["s_edge"]),
         )
 
     to_left, to_right = x_edges()
@@ -367,13 +367,8 @@
     def _():
         to_right.start()
 
-    @pl.when(jnp.logical_not(has_left))
-    def _():
-        xh[0] = jnp.zeros((EDGE, D), BF)
-
-    @pl.when(jnp.logical_not(has_right))
-    def _():
-        xh[1] = jnp.zeros((EDGE, D), BF)
+    xh[0, 0 : EDGE - NEAR, :] = jnp.zeros((EDGE - NEAR, D), BF)
+    xh[1, NEAR:EDGE, :] = jnp.zeros((EDGE - NEAR, D), BF)
 
     first_block = y * (ROWS // EDGE)
     count = segments.shape[0]
@@ -429,15 +424,27 @@
     @pl.when(has_left)
     def _():
         to_left.wait_send()
-        to_right.wait_recv() if Y == 1 else edge((), 1, patches.at[pl.ds(0, EDGE)], xh.at[0], r["s_edge"]).wait_recv()
+        to_right.wait_recv()
 
     @pl.when(has_right)
     def _():
         to_right.wait_send()
-        edge((), 0, patches.at[pl.ds(0, EDGE)], xh.at[1], r["s_edge"]).wait_recv()
+        to_left.wait_recv()
 
     def edge_rows(i, _):
-        project(xh[i], pl.multiple_of(i * (ROWS + EDGE), EDGE), False, 0)
+        at = pl.multiple_of(i * (ROWS + EDGE), EDGE)
+        present = jnp.where(i == 0, y, Y - 1 - y) > 0
+
+        @pl.when(present)
+        def _():
+            project(xh[i], at, False, 0)
+
+        @pl.when(jnp.logical_not(present))
+        def _():
+            r["k"][pl.ds(at, EDGE), :] = jnp.zeros((EDGE, D), BF)
+            r["v"][pl.ds(at, EDGE), :] = jnp.zeros((EDGE, D), BF)
+            r["vT"][:, pl.ds(at, EDGE)] = jnp.zeros((D, EDGE), BF)
+
         return 0
 
     lax.fori_loop(0, 2, edge_rows, 0)

time: 111 us -> 109 us (0.982)
  Pallas kernels: 110 us -> 108 us
    pallas_call x1, Pallas kernels: 105 us -> 104 us  [layer(): pl.pallas_call(functools.partial(layer_kernel, g, names), out_shape=tuple...]
where the time goes in v5:
time: 109 us
  Pallas kernels  108 us (99%)
    pallas_call x1, Pallas kernels, layer(): pl.pallas_call(functools.partial(layer_kernel, g, names), out_shape=tuple...  104 us
    pallas_call x1, Pallas kernels, hand_over(): pl.pallas_call(functools.partial(hand_over_kernel, g), out_shape=tuple((j...  4.26 us

profile of v5, /device:TPU:0, one launch (start us, length us, event | category | flops | bytes accessed | tf_op | source)
XLA Modules:
  0.0 109.1 jit_solution(2715540818708768252)
XLA Ops:
  0.7 104.1 %shard_map.254 = (bf16[512,768]{1,0:T(8,128)(2,1)}, bf16[512,768]{1,0:T(8,128)(2,1)}, f32[48,2304]{1,0:T(8,128)}, f32[48,768]{1,0:T(8,128)}, f32[48,3072]{1,0:T(...) custom-call(bf16[512,768]{1,0:T(8,128)(2,1)} %bitcast.5, ...), custom_call_target="tpu_custom_call" | custom-call | tf_op jit(solution)/shard_map/pallas_call | solution.py:900
  104.8 4.3 %shard_map.255 = (bf16[512,768]{1,0:T(8,128)(2,1)}, bf16[512,768]{1,0:T(8,128)(2,1)}, f32[48]{0:T(128)}, f32[48]{0:T(128)}, f32[48,2304]{1,0:T(8,128)}, /*index=...) custom-call(bf16[512,768]{1,0:T(8,128)(2,1)} %get-tuple-element.37.o, ...), custom_call_target="tpu_custom_call" | custom-call | tf_op jit(solution)/shard_map/pallas_call | solution.py:941

commit v6 on v5

--- a/solution.py
+++ b/solution.py
@@ -470,28 +470,30 @@
         mixed = nn(r["vT"][at, keys], probs)
         r["attT"][at, own] = jnp.where(top, mixed[:, :128], mixed[:, 128:]).astype(BF)
 
-    def attend(p, _):
-        scores = scores_of(p, 0)
+    def attend(i, _):
+        blocks = [(2 * i + pair, b) for pair in range(2) for b in range(4)]
+        scores = scores_of(*blocks[0])
         before = None
-        for b in range(4):
-            following = scores_of(p, b + 1) if b < 3 else None
+        for k, (p, b) in enumerate(blocks):
+            following = scores_of(*blocks[k + 1]) if k + 1 < len(blocks) else None
             probs = probs_of(b, scores)
-            if b > 0:
-                mix(p, b - 1, before)
+            if k > 0:
+                mix(*blocks[k - 1], before)
             before, scores = probs, following
-        mix(p, 3, before)
+        mix(*blocks[-1], before)
         return 0
 
-    lax.fori_loop(0, PAIRS, attend, 0)
+    lax.fori_loop(0, PAIRS // 2, attend, 0)
 
     load_wo.wait()
     mid, total, n2, n2T = r["mid"], r["total"], r["n2"], r["n2T"]
     middle_gain, middle_shift = r["middle_gain"][...], r["middle_shift"][...]
 
-    def finish_attention(i, _):
-        at = pl.ds(pl.multiple_of(i * 256, 256), 256)
-        mixed = r["attT"][:, at].T
-        middle = x[at, :].astype(F32) + nn(mixed, r["wo"][...]) + r["output_bias"][...]
+    halves = [pl.ds(i * 256, 256) for i in range(2)]
+    middles = [
+        x[at, :].astype(F32) + nn(r["attT"][:, at].T, r["wo"][...]) + r["output_bias"][...] for at in halves
+    ]
+    for at, middle in zip(halves, middles):
         mid[at, :] = middle
         total[at, :] = middle + r["reduce_bias"][...]
         normal, _ = stats(middle)
@@ -499,9 +501,6 @@
         n2[at, :] = low
         n2T[:, at] = low.T
         r["dn"][at, :] = jnp.zeros((256, D), F32)
-        return 0
-
-    lax.fori_loop(0, 2, finish_attention, 0)
     load_dy.wait()
 
     def feed_forward(i, _):

time: 109 us -> 109 us (level)
  no operation moved by 1% of the time
where the time goes in v6:
time: 109 us; the launch traced here: 108 us
  Pallas kernels  108 us (99%)
    pallas_call x1, Pallas kernels, layer(): pl.pallas_call(functools.partial(layer_kernel, g, names), out_shape=tuple...  103 us
    pallas_call x1, Pallas kernels, hand_over(): pl.pallas_call(functools.partial(hand_over_kernel, g), out_shape=tuple((j...  4.26 us

profile of v6, /device:TPU:0, one launch (start us, length us, event | category | flops | bytes accessed | tf_op | source)
XLA Modules:
  0.0 108.5 jit_solution(3415776715028824572)
XLA Ops:
  0.7 103.4 %shard_map.254 = (bf16[512,768]{1,0:T(8,128)(2,1)}, bf16[512,768]{1,0:T(8,128)(2,1)}, f32[48,2304]{1,0:T(8,128)}, f32[48,768]{1,0:T(8,128)}, f32[48,3072]{1,0:T(...) custom-call(bf16[512,768]{1,0:T(8,128)(2,1)} %bitcast.5, ...), custom_call_target="tpu_custom_call" | custom-call | tf_op jit(solution)/shard_map/pallas_call | solution.py:899
  104.0 4.3 %shard_map.255 = (bf16[512,768]{1,0:T(8,128)(2,1)}, bf16[512,768]{1,0:T(8,128)(2,1)}, f32[48]{0:T(128)}, f32[48]{0:T(128)}, f32[48,2304]{1,0:T(8,128)}, /*index=...) custom-call(bf16[512,768]{1,0:T(8,128)(2,1)} %get-tuple-element.37.o, ...), custom_call_target="tpu_custom_call" | custom-call | tf_op jit(solution)/shard_map/pallas_call | solution.py:940

commit v7 on v6

--- a/solution.py
+++ b/solution.py
@@ -386,6 +386,7 @@
             r["bias"][b, k * EDGE : (k + 1) * EDGE, :] = jnp.where(keys == own, 0.0, -1e30)
 
     vec[...] = jnp.zeros_like(vec)
+    r["dn"][...] = jnp.zeros((ROWS, D), F32)
     entry_gain, entry_shift = r["entry_gain"][...], r["entry_shift"][...]
     lanes = lax.broadcasted_iota(jnp.int32, (1, D), 1) % 128
     even = lanes < HD
@@ -500,7 +501,6 @@
         low = (normal * middle_gain + middle_shift).astype(BF)
         n2[at, :] = low
         n2T[:, at] = low.T
-        r["dn"][at, :] = jnp.zeros((256, D), F32)
     load_dy.wait()
 
     def feed_forward(i, _):

time: 109 us -> 109 us (level)
  no operation moved by 1% of the time
where the time goes in v7:
time: 109 us; the launch traced here: 108 us
  Pallas kernels  107 us (98%)
    pallas_call x1, Pallas kernels, layer(): pl.pallas_call(functools.partial(layer_kernel, g, names), out_shape=tuple...  103 us
    pallas_call x1, Pallas kernels, hand_over(): pl.pallas_call(functools.partial(hand_over_kernel, g), out_shape=tuple((j...  4.26 us

profile of v7, /device:TPU:0, one launch (start us, length us, event | category | flops | bytes accessed | tf_op | source)
XLA Modules:
  0.0 108.3 jit_solution(15213988251923485622)
XLA Ops:
  0.7 103.2 %shard_map.254 = (bf16[512,768]{1,0:T(8,128)(2,1)}, bf16[512,768]{1,0:T(8,128)(2,1)}, f32[48,2304]{1,0:T(8,128)}, f32[48,768]{1,0:T(8,128)}, f32[48,3072]{1,0:T(...) custom-call(bf16[512,768]{1,0:T(8,128)(2,1)} %bitcast.5, ...), custom_call_target="tpu_custom_call" | custom-call | tf_op jit(solution)/shard_map/pallas_call | solution.py:899
  103.9 4.3 %shard_map.255 = (bf16[512,768]{1,0:T(8,128)(2,1)}, bf16[512,768]{1,0:T(8,128)(2,1)}, f32[48]{0:T(128)}, f32[48]{0:T(128)}, f32[48,2304]{1,0:T(8,128)}, /*index=...) custom-call(bf16[512,768]{1,0:T(8,128)(2,1)} %get-tuple-element.37.o, ...), custom_call_target="tpu_custom_call" | custom-call | tf_op jit(solution)/shard_map/pallas_call | solution.py:940
